TPU v7x, 32 devices: a whole 2x2x4 slice. The times are simulated.
32 devices in a mesh: tile: 8 (over z, core), depth: 4 (over y, x).
Axes of the slice: x: 2, y: 2, z: 4, core: 2. Of those that a mesh axis runs over, the one named last changes fastest.
Arguments:
- velocity: float32 [3, 32, 64, 128], P(None, 'tile', 'depth'), may hold values from -6 to 6
- stress: float32 [6, 32, 64, 128], P(None, 'tile', 'depth'), may hold values from -6 to 6
- memory: float32 [18, 32, 64, 128], P(None, 'tile', 'depth'), may hold values from -3 to 3
- buoyancy: float32 [32, 64, 128], P('tile', 'depth'), may hold values from 0.5 to 1.5
- lame: float32 [2, 32, 64, 128], P(None, 'tile', 'depth'), may hold values from 0.5 to 1.5
- qinv: float32 [2, 32, 64, 128], P(None, 'tile', 'depth'), may hold values from 0.05 to 0.5
- relax: float32 [3], replicated, may hold values from 0.1 to 0.9
- fwd_strain: bfloat16 [4, 6, 32, 64, 128], P(None, None, 'tile', 'depth'), may hold values from -6 to 6
- residual: float32 [32, 3, 1024], P(None, None, 'tile'), may hold values from -6 to 6
- station_owner: int32 [1024, 1], P('tile'), may hold values from 0 to 7; in each aligned block of 128 rows (0 to 127, 128 to 255, ...) at most 64 rows name the same one
- station_cell: int32 [1024], P('tile'), may hold values from 0 to 511
- time_index: int32 [4], replicated, may hold values from 0 to 31
Outputs:
- velocity_out: float32 [3, 32, 64, 128], P(None, 'tile', 'depth')
- stress_out: float32 [6, 32, 64, 128], P(None, 'tile', 'depth')
- memory_out: float32 [18, 32, 64, 128], P(None, 'tile', 'depth')
- kernel_q: float32 [32, 64, 128], P('tile', 'depth')
Inputs may be any that keep to these rules, and one draw needn't show every extreme that they name: `station_owner`: in each aligned block of 128 stations (the stations of one tile index) no tile is named by more than 64 stations, a bound that some block reaches; every tile is named by some station.
All inputs are finite; a program needn't handle non-finite values.
Results may differ from a plain program's by a relative error of at most 0.0004.
Values sent between devices are 32-bit elements; how exact they have to be, the bound alone decides.
A program may use at most 64 MiB of HBM per device.

v0:
```python
import jax
import jax.numpy as jnp
from jax import lax
from jax.sharding import PartitionSpec as P

courant = 0.2
mech_weights = (2.0, 3.0, 4.0)


def with_halo(block, sides, width):
    for axis, dim in sides:
        count = lax.axis_size(axis)
        forward = [(i, i + 1) for i in range(count - 1)]
        backward = [(target, source) for source, target in forward]
        low = lax.ppermute(
            lax.slice_in_dim(block, block.shape[dim] - width, None, axis=dim), axis, forward
        )
        high = lax.ppermute(lax.slice_in_dim(block, 0, width, axis=dim), axis, backward)
        block = jnp.concatenate([low, block, high], axis=dim)
    return block


def along_y(field):
    widths = [(0, 0)] * field.ndim
    widths[3] = (1, 1)
    padded = jnp.pad(field, widths)
    count = field.shape[3]
    return 0.5 * (
        lax.slice_in_dim(padded, 2, count + 2, axis=3) - lax.slice_in_dim(padded, 0, count, axis=3)
    )


def divergence(padded):
    sx = 0.5 * (padded[:, 2:, 1:-1, :] - padded[:, :-2, 1:-1, :])
    sz = 0.5 * (padded[:, 1:-1, 2:, :] - padded[:, 1:-1, :-2, :])
    sy = along_y(padded[:, 1:-1, 1:-1, :])
    return jnp.stack([sx[0] + sy[3] + sz[4], sx[3] + sy[1] + sz[5], sx[4] + sy[5] + sz[2]])


def per_device(
    velocity,
    stress,
    memory,
    buoyancy,
    lame,
    qinv,
    relax,
    fwd_strain,
    residual,
    station_owner,
    station_cell,
    time_index,
):
    cells_x = velocity.shape[1]
    cells_z = velocity.shape[2]
    cells_y = velocity.shape[3]
    surface = cells_x * cells_y
    steps = fwd_strain.shape[0]
    mechs = relax.shape[0]
    owners = station_owner[:, 0]
    listed = owners.shape[0]
    rows = jnp.take(residual, time_index, axis=0).reshape(steps * 3, listed)
    my_tile = lax.axis_index("tile")
    all_rows, all_owners, all_cells = (
        lax.all_gather(rows, "tile", axis=1, tiled=True),
        lax.all_gather(owners, "tile", axis=0, tiled=True),
        lax.all_gather(station_cell, "tile", axis=0, tiled=True),
    )
    target = jnp.where(all_owners == my_tile, all_cells, surface)
    inject_all = jnp.zeros((steps * 3, surface + 1), jnp.float32).at[:, target].add(all_rows)
    inject_all = inject_all[:, :surface]
    inject_all = inject_all.reshape(steps, 3, cells_x, cells_y)
    at_surface = (lax.axis_index("depth") == 0).astype(jnp.float32)
    surface_buoy = at_surface * buoyancy[None, :, 0, :]
    lam = lame[0]
    shear = lame[1]
    kappa = lam + 2.0 / 3.0 * shear
    diagonal = jnp.array([1.0, 1.0, 1.0, 0.0, 0.0, 0.0], dtype=jnp.float32).reshape(6, 1, 1, 1)
    weights = jnp.array(mech_weights, dtype=jnp.float32)
    keep = (1.0 - relax).reshape(mechs, 1, 1, 1, 1)
    push = (relax * weights).reshape(mechs, 1, 1, 1, 1)
    kernel = jnp.zeros(buoyancy.shape, jnp.float32)
    for step in range(steps):
        velocity = velocity.at[:, :, 0, :].add(surface_buoy * inject_all[step])
        padded = with_halo(stress, (("tile", 1), ("depth", 2)), 1)
        velocity = velocity + courant * buoyancy[None] * divergence(padded)
        framed = with_halo(velocity, (("tile", 1), ("depth", 2)), 1)
        gx = 0.5 * (framed[:, 2:, 1:-1, :] - framed[:, :-2, 1:-1, :])
        gz = 0.5 * (framed[:, 1:-1, 2:, :] - framed[:, 1:-1, :-2, :])
        gy = along_y(velocity)
        strain = jnp.stack(
            [
                gx[0],
                gy[1],
                gz[2],
                0.5 * (gy[0] + gx[1]),
                0.5 * (gz[0] + gx[2]),
                0.5 * (gz[1] + gy[2]),
            ]
        )
        theta = strain[0] + strain[1] + strain[2]
        deviator = strain - diagonal * (theta / 3.0)[None]
        force = (
            2.0 * shear[None] * qinv[0][None] * deviator
            + diagonal * (kappa * qinv[1] * theta)[None]
        )
        mems = memory.reshape(mechs, 6, cells_x, cells_z, cells_y)
        mems = keep * mems - push * force[None]
        stress = stress + courant * (
            diagonal * (lam * theta)[None] + 2.0 * shear[None] * strain + jnp.sum(mems, axis=0)
        )
        kernel = kernel + courant * jnp.sum(
            mems * fwd_strain[step].astype(jnp.float32)[None], axis=(0, 1)
        )
        memory = mems.reshape(mechs * 6, cells_x, cells_z, cells_y)
    return (velocity, stress, memory, kernel)


def solution(mesh):
    in_specs = (
        P(None, "tile", "depth", None),
        P(None, "tile", "depth", None),
        P(None, "tile", "depth", None),
        P("tile", "depth", None),
        P(None, "tile", "depth", None),
        P(None, "tile", "depth", None),
        P(),
        P(None, None, "tile", "depth", None),
        P(None, None, "tile"),
        P("tile", None),
        P("tile"),
        P(),
    )
    out_specs = (
        P(None, "tile", "depth", None),
        P(None, "tile", "depth", None),
        P(None, "tile", "depth", None),
        P("tile", "depth", None),
    )
    return jax.shard_map(
        per_device, mesh=mesh, in_specs=in_specs, out_specs=out_specs, check_vma=False
    )
```

profile of v0, /device:TPU:12, one launch (start us, length us, event | category | flops | bytes accessed | tf_op | source)
XLA Modules:
  0.0 178.6 jit_solution(16435187345233080249)
XLA Ops:
  0.7 0.9 copy.61
  1.6 1.9 %collective-permute-start = (f32[6,1,16,128]{3,2,1,0:T(8,128)S(1)}, f32[6,1,16,128]{3,2,1,0:T(8,128)S(1)}, u32[]{:S(2)}, u32[]{:S(2)}) collective-permute-start(f32[6,1,16,128]{3,2,1,0:T(8,128)S(1)} %get-tuple-element.119), channel_id=1, source_target_pairs={{4,0},{8,4},{12,8},{16,12},{20,16},{24,20},{28,24},{5,1},{9,5},{13... | collective-permute-start | bytes 147464 | tf_op jit(solution)/shard_map/ppermute | solution.py:18
  3.6 2.4 %collective-permute-start.1 = (f32[6,1,16,128]{3,2,1,0:T(8,128)S(1)}, f32[6,1,16,128]{3,2,1,0:T(8,128)S(1)}, u32[]{:S(2)}, u32[]{:S(2)}) collective-permute-start(f32[6,1,16,128]{3,2,1,0:T(8,128)S(1)} %get-tuple-element.120), channel_id=1, source_target_pairs={{0,4},{4,8},{8,12},{12,16},{16,20},{20,24},{24,28},{1,5},{5,9},{9,... | collective-permute-start | bytes 147464 | tf_op jit(solution)/shard_map/ppermute | solution.py:15
  6.2 0.6 gather_fusion
  6.9 9.0 %all-gather = s32[1024,1]{0,1:T(1,128)S(1)} all-gather(s32[128,1]{0,1:T(1,128)S(1)} %copy-done.9), channel_id=2, replica_groups=mesh['tile'=8,'depth'=4] {'tile'}, dimensions={0}, use_global_device_ids=true | all-gather | bytes 4608 | tf_op jit(solution)/shard_map/all_gather | solution.py:66
  15.9 0.7 copy-done.10
  16.5 11.7 %all-gather.1 = s32[8,1,128]{2,1,0:T(1,128)S(1)} all-gather(s32[1,1,128]{2,1,0:T(1,128)S(1)} %bitcast.119), channel_id=1, replica_groups=mesh['tile'=8,'depth'=4] {'tile'}, dimensions={0}, use_global_device_ids=true | all-gather | bytes 4608 | tf_op jit(solution)/shard_map/all_gather | solution.py:67
  28.3 12.2 %all_gather.11 = f32[12,1024]{1,0:T(8,128)S(1)} all-gather(f32[12,128]{1,0:T(8,128)S(1)} %broadcast_select_fusion), channel_id=1, replica_groups=mesh['tile'=8,'depth'=4] {'tile'}, dimensions={1}, use_global_device_ids=true | all-gather | bytes 55296 | tf_op jit(solution)/shard_map/all_gather | solution.py:65
  40.4 0.2 copy.29
  40.7 6.9 %scatter_custom_fusion = f32[12,513]{0,1:T(8,128)S(1)} fusion(s32[1024]{0:T(1024)S(1)} %compare_select_fusion, f32[1024,12]{1,0:T(8,128)S(1)} %copy.29, f32[]{:T(128)} %constant.131.clone.1), kind=kCustom, calls=%fused_computation.100 | custom fusion | flops 12288 | bytes 24628 | tf_op jit(solution)/shard_map/scatter-add | solution.py:70
  47.6 0.3 fusion.79
  48.3 3.3 %collective-permute-start.2 = (f32[6,6,1,128]{3,2,1,0:T(1,128)S(1)}, f32[6,6,1,128]{3,2,1,0:T(1,128)S(1)}, u32[]{:S(2)}, u32[]{:S(2)}) collective-permute-start(f32[6,6,1,128]{3,2,1,0:T(1,128)S(1)} %get-tuple-element.97), channel_id=1, source_target_pairs={{1,0},{2,1},{3,2},{5,4},{6,5},{7,6},{9,8},{10,9},{11,10},{13,12},{... | collective-permute-start | bytes 55304 | tf_op jit(solution)/shard_map/ppermute | solution.py:18
  51.6 2.5 %collective-permute-start.3 = (f32[6,6,1,128]{3,2,1,0:T(1,128)S(1)}, f32[6,6,1,128]{3,2,1,0:T(1,128)S(1)}, u32[]{:S(2)}, u32[]{:S(2)}) collective-permute-start(f32[6,6,1,128]{3,2,1,0:T(1,128)S(1)} %get-tuple-element.98), channel_id=1, source_target_pairs={{0,1},{1,2},{2,3},{4,5},{5,6},{6,7},{8,9},{9,10},{10,11},{12,13},{... | collective-permute-start | bytes 55304 | tf_op jit(solution)/shard_map/ppermute | solution.py:15
  54.2 4.0 %collective-permute-done.3 = f32[6,6,1,128]{3,2,1,0:T(1,128)S(1)} collective-permute-done((f32[6,6,1,128]{3,2,1,0:T(1,128)S(1)}, f32[6,6,1,128]{3,2,1,0:T(1,128)S(1)}, u32[]{:S(2)}, u32[]{:S(2)}) %collective-permute-start.3) | collective-permute-done | bytes 18464 | tf_op jit(solution)/shard_map/ppermute | solution.py:15
  58.3 2.8 %collective-permute-start.4 = (f32[3,1,16,128]{3,2,1,0:T(8,128)S(1)}, f32[3,1,16,128]{3,2,1,0:T(8,128)S(1)}, u32[]{:S(2)}, u32[]{:S(2)}) collective-permute-start(f32[3,1,16,128]{3,2,1,0:T(8,128)S(1)} %get-tuple-element.148), channel_id=1, source_target_pairs={{4,0},{8,4},{12,8},{16,12},{20,16},{24,20},{28,24},{5,1},{9,5},{13... | collective-permute-start | bytes 73736 | tf_op jit(solution)/shard_map/ppermute | solution.py:18
  61.2 1.9 %collective-permute-start.5 = (f32[3,1,16,128]{3,2,1,0:T(8,128)S(1)}, f32[3,1,16,128]{3,2,1,0:T(8,128)S(1)}, u32[]{:S(2)}, u32[]{:S(2)}) collective-permute-start(f32[3,1,16,128]{3,2,1,0:T(8,128)S(1)} %get-tuple-element.149), channel_id=1, source_target_pairs={{0,4},{4,8},{8,12},{12,16},{16,20},{20,24},{24,28},{1,5},{5,9},{9,... | collective-permute-start | bytes 73736 | tf_op jit(solution)/shard_map/ppermute | solution.py:15
  63.1 3.2 %collective-permute-done.5 = f32[3,1,16,128]{3,2,1,0:T(8,128)S(1)} collective-permute-done((f32[3,1,16,128]{3,2,1,0:T(8,128)S(1)}, f32[3,1,16,128]{3,2,1,0:T(8,128)S(1)}, u32[]{:S(2)}, u32[]{:S(2)}) %collective-permute-start.5) | collective-permute-done | bytes 24608 | tf_op jit(solution)/shard_map/ppermute | solution.py:15
  66.4 1.9 %collective-permute-start.6 = (f32[3,6,1,128]{3,2,1,0:T(1,128)S(1)}, f32[3,6,1,128]{3,2,1,0:T(1,128)S(1)}, u32[]{:S(2)}, u32[]{:S(2)}) collective-permute-start(f32[3,6,1,128]{3,2,1,0:T(1,128)S(1)} %get-tuple-element.135), channel_id=1, source_target_pairs={{1,0},{2,1},{3,2},{5,4},{6,5},{7,6},{9,8},{10,9},{11,10},{13,12},{... | collective-permute-start | bytes 27656 | tf_op jit(solution)/shard_map/ppermute | solution.py:18
  68.3 3.9 %collective-permute-start.7 = (f32[3,6,1,128]{3,2,1,0:T(1,128)S(1)}, f32[3,6,1,128]{3,2,1,0:T(1,128)S(1)}, u32[]{:S(2)}, u32[]{:S(2)}) collective-permute-start(f32[3,6,1,128]{3,2,1,0:T(1,128)S(1)} %get-tuple-element.136), channel_id=1, source_target_pairs={{0,1},{1,2},{2,3},{4,5},{5,6},{6,7},{8,9},{9,10},{10,11},{12,13},{... | collective-permute-start | bytes 27656 | tf_op jit(solution)/shard_map/ppermute | solution.py:15
  72.3 2.5 %collective-permute-done.7 = f32[3,6,1,128]{3,2,1,0:T(1,128)S(1)} collective-permute-done((f32[3,6,1,128]{3,2,1,0:T(1,128)S(1)}, f32[3,6,1,128]{3,2,1,0:T(1,128)S(1)}, u32[]{:S(2)}, u32[]{:S(2)}) %collective-permute-start.7) | collective-permute-done | bytes 9248 | tf_op jit(solution)/shard_map/ppermute | solution.py:15
  74.9 0.8 copy-done.4
  75.8 0.8 copy-done.6
  77.1 1.9 %collective-permute-start.9 = (f32[6,1,16,128]{3,2,1,0:T(8,128)S(1)}, f32[6,1,16,128]{3,2,1,0:T(8,128)S(1)}, u32[]{:S(2)}, u32[]{:S(2)}) collective-permute-start(f32[6,1,16,128]{3,2,1,0:T(8,128)S(1)} %get-tuple-element.113), channel_id=1, source_target_pairs={{0,4},{4,8},{8,12},{12,16},{16,20},{20,24},{24,28},{1,5},{5,9},{9,... | collective-permute-start | bytes 147464 | tf_op jit(solution)/shard_map/ppermute | solution.py:15
  79.1 3.6 %collective-permute-start.8 = (f32[6,1,16,128]{3,2,1,0:T(8,128)S(1)}, f32[6,1,16,128]{3,2,1,0:T(8,128)S(1)}, u32[]{:S(2)}, u32[]{:S(2)}) collective-permute-start(f32[6,1,16,128]{3,2,1,0:T(8,128)S(1)} %get-tuple-element.114), channel_id=1, source_target_pairs={{4,0},{8,4},{12,8},{16,12},{20,16},{24,20},{28,24},{5,1},{9,5},{13... | collective-permute-start | bytes 147464 | tf_op jit(solution)/shard_map/ppermute | solution.py:18
  82.8 1.6 collective-permute-done.8
  84.5 1.9 %collective-permute-start.10 = (f32[6,6,1,128]{3,2,1,0:T(1,128)S(1)}, f32[6,6,1,128]{3,2,1,0:T(1,128)S(1)}, u32[]{:S(2)}, u32[]{:S(2)}) collective-permute-start(f32[6,6,1,128]{3,2,1,0:T(1,128)S(1)} %get-tuple-element.95), channel_id=1, source_target_pairs={{1,0},{2,1},{3,2},{5,4},{6,5},{7,6},{9,8},{10,9},{11,10},{13,12},{... | collective-permute-start | bytes 55304 | tf_op jit(solution)/shard_map/ppermute | solution.py:18
  86.4 3.9 %collective-permute-start.11 = (f32[6,6,1,128]{3,2,1,0:T(1,128)S(1)}, f32[6,6,1,128]{3,2,1,0:T(1,128)S(1)}, u32[]{:S(2)}, u32[]{:S(2)}) collective-permute-start(f32[6,6,1,128]{3,2,1,0:T(1,128)S(1)} %get-tuple-element.96), channel_id=1, source_target_pairs={{0,1},{1,2},{2,3},{4,5},{5,6},{6,7},{8,9},{9,10},{10,11},{12,13},{... | collective-permute-start | bytes 55304 | tf_op jit(solution)/shard_map/ppermute | solution.py:15
  90.4 2.5 %collective-permute-done.11 = f32[6,6,1,128]{3,2,1,0:T(1,128)S(1)} collective-permute-done((f32[6,6,1,128]{3,2,1,0:T(1,128)S(1)}, f32[6,6,1,128]{3,2,1,0:T(1,128)S(1)}, u32[]{:S(2)}, u32[]{:S(2)}) %collective-permute-start.11) | collective-permute-done | bytes 18464 | tf_op jit(solution)/shard_map/ppermute | solution.py:15
  93.2 2.5 %collective-permute-start.12 = (f32[3,1,16,128]{3,2,1,0:T(8,128)S(1)}, f32[3,1,16,128]{3,2,1,0:T(8,128)S(1)}, u32[]{:S(2)}, u32[]{:S(2)}) collective-permute-start(f32[3,1,16,128]{3,2,1,0:T(8,128)S(1)} %get-tuple-element.145), channel_id=1, source_target_pairs={{4,0},{8,4},{12,8},{16,12},{20,16},{24,20},{28,24},{5,1},{9,5},{13... | collective-permute-start | bytes 73736 | tf_op jit(solution)/shard_map/ppermute | solution.py:18
  95.7 1.9 %collective-permute-start.13 = (f32[3,1,16,128]{3,2,1,0:T(8,128)S(1)}, f32[3,1,16,128]{3,2,1,0:T(8,128)S(1)}, u32[]{:S(2)}, u32[]{:S(2)}) collective-permute-start(f32[3,1,16,128]{3,2,1,0:T(8,128)S(1)} %get-tuple-element.146), channel_id=1, source_target_pairs={{0,4},{4,8},{8,12},{12,16},{16,20},{20,24},{24,28},{1,5},{5,9},{9,... | collective-permute-start | bytes 73736 | tf_op jit(solution)/shard_map/ppermute | solution.py:15
  97.7 3.2 %collective-permute-done.13 = f32[3,1,16,128]{3,2,1,0:T(8,128)S(1)} collective-permute-done((f32[3,1,16,128]{3,2,1,0:T(8,128)S(1)}, f32[3,1,16,128]{3,2,1,0:T(8,128)S(1)}, u32[]{:S(2)}, u32[]{:S(2)}) %collective-permute-start.13) | collective-permute-done | bytes 24608 | tf_op jit(solution)/shard_map/ppermute | solution.py:15
  100.9 1.9 %collective-permute-start.14 = (f32[3,6,1,128]{3,2,1,0:T(1,128)S(1)}, f32[3,6,1,128]{3,2,1,0:T(1,128)S(1)}, u32[]{:S(2)}, u32[]{:S(2)}) collective-permute-start(f32[3,6,1,128]{3,2,1,0:T(1,128)S(1)} %get-tuple-element.131), channel_id=1, source_target_pairs={{1,0},{2,1},{3,2},{5,4},{6,5},{7,6},{9,8},{10,9},{11,10},{13,12},{... | collective-permute-start | bytes 27656 | tf_op jit(solution)/shard_map/ppermute | solution.py:18
  102.8 3.9 %collective-permute-start.15 = (f32[3,6,1,128]{3,2,1,0:T(1,128)S(1)}, f32[3,6,1,128]{3,2,1,0:T(1,128)S(1)}, u32[]{:S(2)}, u32[]{:S(2)}) collective-permute-start(f32[3,6,1,128]{3,2,1,0:T(1,128)S(1)} %get-tuple-element.132), channel_id=1, source_target_pairs={{0,1},{1,2},{2,3},{4,5},{5,6},{6,7},{8,9},{9,10},{10,11},{12,13},{... | collective-permute-start | bytes 27656 | tf_op jit(solution)/shard_map/ppermute | solution.py:15
  106.8 2.5 %collective-permute-done.15 = f32[3,6,1,128]{3,2,1,0:T(1,128)S(1)} collective-permute-done((f32[3,6,1,128]{3,2,1,0:T(1,128)S(1)}, f32[3,6,1,128]{3,2,1,0:T(1,128)S(1)}, u32[]{:S(2)}, u32[]{:S(2)}) %collective-permute-start.15) | collective-permute-done | bytes 9248 | tf_op jit(solution)/shard_map/ppermute | solution.py:15
  109.6 0.2 fusion.76
  110.0 1.9 %collective-permute-start.17 = (f32[6,1,16,128]{3,2,1,0:T(8,128)S(1)}, f32[6,1,16,128]{3,2,1,0:T(8,128)S(1)}, u32[]{:S(2)}, u32[]{:S(2)}) collective-permute-start(f32[6,1,16,128]{3,2,1,0:T(8,128)S(1)} %get-tuple-element.109), channel_id=1, source_target_pairs={{0,4},{4,8},{8,12},{12,16},{16,20},{20,24},{24,28},{1,5},{5,9},{9,... | collective-permute-start | bytes 147464 | tf_op jit(solution)/shard_map/ppermute | solution.py:15
  111.9 3.6 %collective-permute-start.16 = (f32[6,1,16,128]{3,2,1,0:T(8,128)S(1)}, f32[6,1,16,128]{3,2,1,0:T(8,128)S(1)}, u32[]{:S(2)}, u32[]{:S(2)}) collective-permute-start(f32[6,1,16,128]{3,2,1,0:T(8,128)S(1)} %get-tuple-element.110), channel_id=1, source_target_pairs={{4,0},{8,4},{12,8},{16,12},{20,16},{24,20},{28,24},{5,1},{9,5},{13... | collective-permute-start | bytes 147464 | tf_op jit(solution)/shard_map/ppermute | solution.py:18
  115.7 1.6 collective-permute-done.16
  117.3 1.9 %collective-permute-start.18 = (f32[6,6,1,128]{3,2,1,0:T(1,128)S(1)}, f32[6,6,1,128]{3,2,1,0:T(1,128)S(1)}, u32[]{:S(2)}, u32[]{:S(2)}) collective-permute-start(f32[6,6,1,128]{3,2,1,0:T(1,128)S(1)} %get-tuple-element.91), channel_id=1, source_target_pairs={{1,0},{2,1},{3,2},{5,4},{6,5},{7,6},{9,8},{10,9},{11,10},{13,12},{... | collective-permute-start | bytes 55304 | tf_op jit(solution)/shard_map/ppermute | solution.py:18
  119.2 3.9 %collective-permute-start.19 = (f32[6,6,1,128]{3,2,1,0:T(1,128)S(1)}, f32[6,6,1,128]{3,2,1,0:T(1,128)S(1)}, u32[]{:S(2)}, u32[]{:S(2)}) collective-permute-start(f32[6,6,1,128]{3,2,1,0:T(1,128)S(1)} %get-tuple-element.92), channel_id=1, source_target_pairs={{0,1},{1,2},{2,3},{4,5},{5,6},{6,7},{8,9},{9,10},{10,11},{12,13},{... | collective-permute-start | bytes 55304 | tf_op jit(solution)/shard_map/ppermute | solution.py:15
  123.3 2.5 %collective-permute-done.19 = f32[6,6,1,128]{3,2,1,0:T(1,128)S(1)} collective-permute-done((f32[6,6,1,128]{3,2,1,0:T(1,128)S(1)}, f32[6,6,1,128]{3,2,1,0:T(1,128)S(1)}, u32[]{:S(2)}, u32[]{:S(2)}) %collective-permute-start.19) | collective-permute-done | bytes 18464 | tf_op jit(solution)/shard_map/ppermute | solution.py:15
  126.0 2.5 %collective-permute-start.20 = (f32[3,1,16,128]{3,2,1,0:T(8,128)S(1)}, f32[3,1,16,128]{3,2,1,0:T(8,128)S(1)}, u32[]{:S(2)}, u32[]{:S(2)}) collective-permute-start(f32[3,1,16,128]{3,2,1,0:T(8,128)S(1)} %get-tuple-element.142), channel_id=1, source_target_pairs={{4,0},{8,4},{12,8},{16,12},{20,16},{24,20},{28,24},{5,1},{9,5},{13... | collective-permute-start | bytes 73736 | tf_op jit(solution)/shard_map/ppermute | solution.py:18
  128.6 1.9 %collective-permute-start.21 = (f32[3,1,16,128]{3,2,1,0:T(8,128)S(1)}, f32[3,1,16,128]{3,2,1,0:T(8,128)S(1)}, u32[]{:S(2)}, u32[]{:S(2)}) collective-permute-start(f32[3,1,16,128]{3,2,1,0:T(8,128)S(1)} %get-tuple-element.143), channel_id=1, source_target_pairs={{0,4},{4,8},{8,12},{12,16},{16,20},{20,24},{24,28},{1,5},{5,9},{9,... | collective-permute-start | bytes 73736 | tf_op jit(solution)/shard_map/ppermute | solution.py:15
  130.5 3.2 %collective-permute-done.21 = f32[3,1,16,128]{3,2,1,0:T(8,128)S(1)} collective-permute-done((f32[3,1,16,128]{3,2,1,0:T(8,128)S(1)}, f32[3,1,16,128]{3,2,1,0:T(8,128)S(1)}, u32[]{:S(2)}, u32[]{:S(2)}) %collective-permute-start.21) | collective-permute-done | bytes 24608 | tf_op jit(solution)/shard_map/ppermute | solution.py:15
  133.7 1.9 %collective-permute-start.22 = (f32[3,6,1,128]{3,2,1,0:T(1,128)S(1)}, f32[3,6,1,128]{3,2,1,0:T(1,128)S(1)}, u32[]{:S(2)}, u32[]{:S(2)}) collective-permute-start(f32[3,6,1,128]{3,2,1,0:T(1,128)S(1)} %get-tuple-element.127), channel_id=1, source_target_pairs={{1,0},{2,1},{3,2},{5,4},{6,5},{7,6},{9,8},{10,9},{11,10},{13,12},{... | collective-permute-start | bytes 27656 | tf_op jit(solution)/shard_map/ppermute | solution.py:18
  135.7 3.9 %collective-permute-start.23 = (f32[3,6,1,128]{3,2,1,0:T(1,128)S(1)}, f32[3,6,1,128]{3,2,1,0:T(1,128)S(1)}, u32[]{:S(2)}, u32[]{:S(2)}) collective-permute-start(f32[3,6,1,128]{3,2,1,0:T(1,128)S(1)} %get-tuple-element.128), channel_id=1, source_target_pairs={{0,1},{1,2},{2,3},{4,5},{5,6},{6,7},{8,9},{9,10},{10,11},{12,13},{... | collective-permute-start | bytes 27656 | tf_op jit(solution)/shard_map/ppermute | solution.py:15
  139.6 2.5 %collective-permute-done.23 = f32[3,6,1,128]{3,2,1,0:T(1,128)S(1)} collective-permute-done((f32[3,6,1,128]{3,2,1,0:T(1,128)S(1)}, f32[3,6,1,128]{3,2,1,0:T(1,128)S(1)}, u32[]{:S(2)}, u32[]{:S(2)}) %collective-permute-start.23) | collective-permute-done | bytes 9248 | tf_op jit(solution)/shard_map/ppermute | solution.py:15
  142.5 0.3 fusion.9
  142.9 1.9 %collective-permute-start.25 = (f32[6,1,16,128]{3,2,1,0:T(8,128)S(1)}, f32[6,1,16,128]{3,2,1,0:T(8,128)S(1)}, u32[]{:S(2)}, u32[]{:S(2)}) collective-permute-start(f32[6,1,16,128]{3,2,1,0:T(8,128)S(1)} %get-tuple-element.105), channel_id=1, source_target_pairs={{0,4},{4,8},{8,12},{12,16},{16,20},{20,24},{24,28},{1,5},{5,9},{9,... | collective-permute-start | bytes 147464 | tf_op jit(solution)/shard_map/ppermute | solution.py:15
  144.8 3.6 %collective-permute-start.24 = (f32[6,1,16,128]{3,2,1,0:T(8,128)S(1)}, f32[6,1,16,128]{3,2,1,0:T(8,128)S(1)}, u32[]{:S(2)}, u32[]{:S(2)}) collective-permute-start(f32[6,1,16,128]{3,2,1,0:T(8,128)S(1)} %get-tuple-element.106), channel_id=1, source_target_pairs={{4,0},{8,4},{12,8},{16,12},{20,16},{24,20},{28,24},{5,1},{9,5},{13... | collective-permute-start | bytes 147464 | tf_op jit(solution)/shard_map/ppermute | solution.py:18
  148.6 1.6 collective-permute-done.24
  150.2 1.9 %collective-permute-start.26 = (f32[6,6,1,128]{3,2,1,0:T(1,128)S(1)}, f32[6,6,1,128]{3,2,1,0:T(1,128)S(1)}, u32[]{:S(2)}, u32[]{:S(2)}) collective-permute-start(f32[6,6,1,128]{3,2,1,0:T(1,128)S(1)} %get-tuple-element.87), channel_id=1, source_target_pairs={{1,0},{2,1},{3,2},{5,4},{6,5},{7,6},{9,8},{10,9},{11,10},{13,12},{... | collective-permute-start | bytes 55304 | tf_op jit(solution)/shard_map/ppermute | solution.py:18
  152.1 3.9 %collective-permute-start.27 = (f32[6,6,1,128]{3,2,1,0:T(1,128)S(1)}, f32[6,6,1,128]{3,2,1,0:T(1,128)S(1)}, u32[]{:S(2)}, u32[]{:S(2)}) collective-permute-start(f32[6,6,1,128]{3,2,1,0:T(1,128)S(1)} %get-tuple-element.88), channel_id=1, source_target_pairs={{0,1},{1,2},{2,3},{4,5},{5,6},{6,7},{8,9},{9,10},{10,11},{12,13},{... | collective-permute-start | bytes 55304 | tf_op jit(solution)/shard_map/ppermute | solution.py:15
  156.2 2.5 %collective-permute-done.27 = f32[6,6,1,128]{3,2,1,0:T(1,128)S(1)} collective-permute-done((f32[6,6,1,128]{3,2,1,0:T(1,128)S(1)}, f32[6,6,1,128]{3,2,1,0:T(1,128)S(1)}, u32[]{:S(2)}, u32[]{:S(2)}) %collective-permute-start.27) | collective-permute-done | bytes 18464 | tf_op jit(solution)/shard_map/ppermute | solution.py:15
  159.0 2.7 %collective-permute-start.28 = (f32[3,1,16,128]{3,2,1,0:T(8,128)S(1)}, f32[3,1,16,128]{3,2,1,0:T(8,128)S(1)}, u32[]{:S(2)}, u32[]{:S(2)}) collective-permute-start(f32[3,1,16,128]{3,2,1,0:T(8,128)S(1)} %get-tuple-element.139), channel_id=1, source_target_pairs={{4,0},{8,4},{12,8},{16,12},{20,16},{24,20},{28,24},{5,1},{9,5},{13... | collective-permute-start | bytes 73736 | tf_op jit(solution)/shard_map/ppermute | solution.py:18
  161.6 1.9 %collective-permute-start.29 = (f32[3,1,16,128]{3,2,1,0:T(8,128)S(1)}, f32[3,1,16,128]{3,2,1,0:T(8,128)S(1)}, u32[]{:S(2)}, u32[]{:S(2)}) collective-permute-start(f32[3,1,16,128]{3,2,1,0:T(8,128)S(1)} %get-tuple-element.140), channel_id=1, source_target_pairs={{0,4},{4,8},{8,12},{12,16},{16,20},{20,24},{24,28},{1,5},{5,9},{9,... | collective-permute-start | bytes 73736 | tf_op jit(solution)/shard_map/ppermute | solution.py:15
  163.6 3.2 %collective-permute-done.29 = f32[3,1,16,128]{3,2,1,0:T(8,128)S(1)} collective-permute-done((f32[3,1,16,128]{3,2,1,0:T(8,128)S(1)}, f32[3,1,16,128]{3,2,1,0:T(8,128)S(1)}, u32[]{:S(2)}, u32[]{:S(2)}) %collective-permute-start.29) | collective-permute-done | bytes 24608 | tf_op jit(solution)/shard_map/ppermute | solution.py:15
  166.8 1.9 %collective-permute-start.30 = (f32[3,6,1,128]{3,2,1,0:T(1,128)S(1)}, f32[3,6,1,128]{3,2,1,0:T(1,128)S(1)}, u32[]{:S(2)}, u32[]{:S(2)}) collective-permute-start(f32[3,6,1,128]{3,2,1,0:T(1,128)S(1)} %get-tuple-element.123), channel_id=1, source_target_pairs={{1,0},{2,1},{3,2},{5,4},{6,5},{7,6},{9,8},{10,9},{11,10},{13,12},{... | collective-permute-start | bytes 27656 | tf_op jit(solution)/shard_map/ppermute | solution.py:18
  168.7 3.9 %collective-permute-start.31 = (f32[3,6,1,128]{3,2,1,0:T(1,128)S(1)}, f32[3,6,1,128]{3,2,1,0:T(1,128)S(1)}, u32[]{:S(2)}, u32[]{:S(2)}) collective-permute-start(f32[3,6,1,128]{3,2,1,0:T(1,128)S(1)} %get-tuple-element.124), channel_id=1, source_target_pairs={{0,1},{1,2},{2,3},{4,5},{5,6},{6,7},{8,9},{9,10},{10,11},{12,13},{... | collective-permute-start | bytes 27656 | tf_op jit(solution)/shard_map/ppermute | solution.py:15
  173.0 2.1 %collective-permute-done.31 = f32[3,6,1,128]{3,2,1,0:T(1,128)S(1)} collective-permute-done((f32[3,6,1,128]{3,2,1,0:T(1,128)S(1)}, f32[3,6,1,128]{3,2,1,0:T(1,128)S(1)}, u32[]{:S(2)}, u32[]{:S(2)}) %collective-permute-start.31) | collective-permute-done | bytes 9248 | tf_op jit(solution)/shard_map/ppermute | solution.py:15
  175.5 0.3 subtract_reduce_fusion
  175.9 0.8 multiply_add_fusion
  176.6 1.3 fusion.2
  178.0 0.6 add_multiply_fusion
  (142 shorter events, 4.4 us)
Async XLA Ops:
  0.6 5.6 %copy-start = (f32[32,3,128]{2,0,1:T(8,128)S(1)}, f32[32,3,128]{2,0,1:T(8,128)}, u32[]{:S(2)}) copy-start(f32[32,3,128]{2,0,1:T(8,128)} %param.30) | copy-start | bytes 147460
  0.6 1.0 copy-start.2
  1.6 46.4 %collective-permute-start = (f32[6,1,16,128]{3,2,1,0:T(8,128)S(1)}, f32[6,1,16,128]{3,2,1,0:T(8,128)S(1)}, u32[]{:S(2)}, u32[]{:S(2)}) collective-permute-start(f32[6,1,16,128]{3,2,1,0:T(8,128)S(1)} %get-tuple-element.119), channel_id=1, source_target_pairs={{4,0},{8,4},{12,8},{16,12},{20,16},{24,20},{28,24},{5,1},{9,5},{13... | collective-permute-start | bytes 147464 | tf_op jit(solution)/shard_map/ppermute | solution.py:18
  3.6 2.4 %copy-start.13 = (s32[4]{0:T(128)S(1)}, s32[4]{0:T(128)}, u32[]{:S(2)}) copy-start(s32[4]{0:T(128)} %param.33) | copy-start | bytes 52
  3.6 44.4 %collective-permute-start.1 = (f32[6,1,16,128]{3,2,1,0:T(8,128)S(1)}, f32[6,1,16,128]{3,2,1,0:T(8,128)S(1)}, u32[]{:S(2)}, u32[]{:S(2)}) collective-permute-start(f32[6,1,16,128]{3,2,1,0:T(8,128)S(1)} %get-tuple-element.120), channel_id=1, source_target_pairs={{0,4},{4,8},{8,12},{12,16},{16,20},{20,24},{24,28},{1,5},{5,9},{9,... | collective-permute-start | bytes 147464 | tf_op jit(solution)/shard_map/ppermute | solution.py:15
  6.2 0.7 copy-start.9
  6.8 21.4 %copy-start.7 = (f32[4,16,128]{2,1,0:T(8,128)S(1)}, f32[4,16,128]{2,1,0:T(8,128)}, u32[]{:S(2)}) copy-start(f32[4,16,128]{2,1,0:T(8,128)} %param.25) | copy-start | bytes 98308
  15.9 0.7 copy-start.10
  48.3 5.9 %collective-permute-start.2 = (f32[6,6,1,128]{3,2,1,0:T(1,128)S(1)}, f32[6,6,1,128]{3,2,1,0:T(1,128)S(1)}, u32[]{:S(2)}, u32[]{:S(2)}) collective-permute-start(f32[6,6,1,128]{3,2,1,0:T(1,128)S(1)} %get-tuple-element.97), channel_id=1, source_target_pairs={{1,0},{2,1},{3,2},{5,4},{6,5},{7,6},{9,8},{10,9},{11,10},{13,12},{... | collective-permute-start | bytes 55304 | tf_op jit(solution)/shard_map/ppermute | solution.py:18
  51.6 6.6 %collective-permute-start.3 = (f32[6,6,1,128]{3,2,1,0:T(1,128)S(1)}, f32[6,6,1,128]{3,2,1,0:T(1,128)S(1)}, u32[]{:S(2)}, u32[]{:S(2)}) collective-permute-start(f32[6,6,1,128]{3,2,1,0:T(1,128)S(1)} %get-tuple-element.98), channel_id=1, source_target_pairs={{0,1},{1,2},{2,3},{4,5},{5,6},{6,7},{8,9},{9,10},{10,11},{12,13},{... | collective-permute-start | bytes 55304 | tf_op jit(solution)/shard_map/ppermute | solution.py:15
  58.3 4.8 %collective-permute-start.4 = (f32[3,1,16,128]{3,2,1,0:T(8,128)S(1)}, f32[3,1,16,128]{3,2,1,0:T(8,128)S(1)}, u32[]{:S(2)}, u32[]{:S(2)}) collective-permute-start(f32[3,1,16,128]{3,2,1,0:T(8,128)S(1)} %get-tuple-element.148), channel_id=1, source_target_pairs={{4,0},{8,4},{12,8},{16,12},{20,16},{24,20},{28,24},{5,1},{9,5},{13... | collective-permute-start | bytes 73736 | tf_op jit(solution)/shard_map/ppermute | solution.py:18
  61.2 5.1 %collective-permute-start.5 = (f32[3,1,16,128]{3,2,1,0:T(8,128)S(1)}, f32[3,1,16,128]{3,2,1,0:T(8,128)S(1)}, u32[]{:S(2)}, u32[]{:S(2)}) collective-permute-start(f32[3,1,16,128]{3,2,1,0:T(8,128)S(1)} %get-tuple-element.149), channel_id=1, source_target_pairs={{0,4},{4,8},{8,12},{12,16},{16,20},{20,24},{24,28},{1,5},{5,9},{9,... | collective-permute-start | bytes 73736 | tf_op jit(solution)/shard_map/ppermute | solution.py:15
  66.3 5.9 %copy-start.11 = (f32[3]{0:T(128)S(1)}, f32[3]{0:T(128)}, u32[]{:S(2)}) copy-start(f32[3]{0:T(128)} %param.28) | copy-start | bytes 40
  66.3 5.9 %copy-start.12 = (f32[3]{0:T(128)S(1)}, f32[3]{0:T(128)}, u32[]{:S(2)}) copy-start(f32[3]{0:T(128)} %constant.146.clone) | copy-start | bytes 40
  66.4 5.9 %collective-permute-start.6 = (f32[3,6,1,128]{3,2,1,0:T(1,128)S(1)}, f32[3,6,1,128]{3,2,1,0:T(1,128)S(1)}, u32[]{:S(2)}, u32[]{:S(2)}) collective-permute-start(f32[3,6,1,128]{3,2,1,0:T(1,128)S(1)} %get-tuple-element.135), channel_id=1, source_target_pairs={{1,0},{2,1},{3,2},{5,4},{6,5},{7,6},{9,8},{10,9},{11,10},{13,12},{... | collective-permute-start | bytes 27656 | tf_op jit(solution)/shard_map/ppermute | solution.py:18
  68.3 6.5 %collective-permute-start.7 = (f32[3,6,1,128]{3,2,1,0:T(1,128)S(1)}, f32[3,6,1,128]{3,2,1,0:T(1,128)S(1)}, u32[]{:S(2)}, u32[]{:S(2)}) collective-permute-start(f32[3,6,1,128]{3,2,1,0:T(1,128)S(1)} %get-tuple-element.136), channel_id=1, source_target_pairs={{0,1},{1,2},{2,3},{4,5},{5,6},{6,7},{8,9},{9,10},{10,11},{12,13},{... | collective-permute-start | bytes 27656 | tf_op jit(solution)/shard_map/ppermute | solution.py:15
  74.9 0.8 copy-start.4
  75.7 0.8 copy-start.6
  75.7 0.9 copy-start.8
  75.8 1.1 copy-start.1
  77.1 5.7 %collective-permute-start.9 = (f32[6,1,16,128]{3,2,1,0:T(8,128)S(1)}, f32[6,1,16,128]{3,2,1,0:T(8,128)S(1)}, u32[]{:S(2)}, u32[]{:S(2)}) collective-permute-start(f32[6,1,16,128]{3,2,1,0:T(8,128)S(1)} %get-tuple-element.113), channel_id=1, source_target_pairs={{0,4},{4,8},{8,12},{12,16},{16,20},{20,24},{24,28},{1,5},{5,9},{9,... | collective-permute-start | bytes 147464 | tf_op jit(solution)/shard_map/ppermute | solution.py:15
  79.1 5.4 %collective-permute-start.8 = (f32[6,1,16,128]{3,2,1,0:T(8,128)S(1)}, f32[6,1,16,128]{3,2,1,0:T(8,128)S(1)}, u32[]{:S(2)}, u32[]{:S(2)}) collective-permute-start(f32[6,1,16,128]{3,2,1,0:T(8,128)S(1)} %get-tuple-element.114), channel_id=1, source_target_pairs={{4,0},{8,4},{12,8},{16,12},{20,16},{24,20},{28,24},{5,1},{9,5},{13... | collective-permute-start | bytes 147464 | tf_op jit(solution)/shard_map/ppermute | solution.py:18
  84.5 5.9 %collective-permute-start.10 = (f32[6,6,1,128]{3,2,1,0:T(1,128)S(1)}, f32[6,6,1,128]{3,2,1,0:T(1,128)S(1)}, u32[]{:S(2)}, u32[]{:S(2)}) collective-permute-start(f32[6,6,1,128]{3,2,1,0:T(1,128)S(1)} %get-tuple-element.95), channel_id=1, source_target_pairs={{1,0},{2,1},{3,2},{5,4},{6,5},{7,6},{9,8},{10,9},{11,10},{13,12},{... | collective-permute-start | bytes 55304 | tf_op jit(solution)/shard_map/ppermute | solution.py:18
  86.4 6.6 %collective-permute-start.11 = (f32[6,6,1,128]{3,2,1,0:T(1,128)S(1)}, f32[6,6,1,128]{3,2,1,0:T(1,128)S(1)}, u32[]{:S(2)}, u32[]{:S(2)}) collective-permute-start(f32[6,6,1,128]{3,2,1,0:T(1,128)S(1)} %get-tuple-element.96), channel_id=1, source_target_pairs={{0,1},{1,2},{2,3},{4,5},{5,6},{6,7},{8,9},{9,10},{10,11},{12,13},{... | collective-permute-start | bytes 55304 | tf_op jit(solution)/shard_map/ppermute | solution.py:15
  93.2 4.5 %collective-permute-start.12 = (f32[3,1,16,128]{3,2,1,0:T(8,128)S(1)}, f32[3,1,16,128]{3,2,1,0:T(8,128)S(1)}, u32[]{:S(2)}, u32[]{:S(2)}) collective-permute-start(f32[3,1,16,128]{3,2,1,0:T(8,128)S(1)} %get-tuple-element.145), channel_id=1, source_target_pairs={{4,0},{8,4},{12,8},{16,12},{20,16},{24,20},{28,24},{5,1},{9,5},{13... | collective-permute-start | bytes 73736 | tf_op jit(solution)/shard_map/ppermute | solution.py:18
  95.7 5.1 %collective-permute-start.13 = (f32[3,1,16,128]{3,2,1,0:T(8,128)S(1)}, f32[3,1,16,128]{3,2,1,0:T(8,128)S(1)}, u32[]{:S(2)}, u32[]{:S(2)}) collective-permute-start(f32[3,1,16,128]{3,2,1,0:T(8,128)S(1)} %get-tuple-element.146), channel_id=1, source_target_pairs={{0,4},{4,8},{8,12},{12,16},{16,20},{20,24},{24,28},{1,5},{5,9},{9,... | collective-permute-start | bytes 73736 | tf_op jit(solution)/shard_map/ppermute | solution.py:15
  100.9 5.9 %collective-permute-start.14 = (f32[3,6,1,128]{3,2,1,0:T(1,128)S(1)}, f32[3,6,1,128]{3,2,1,0:T(1,128)S(1)}, u32[]{:S(2)}, u32[]{:S(2)}) collective-permute-start(f32[3,6,1,128]{3,2,1,0:T(1,128)S(1)} %get-tuple-element.131), channel_id=1, source_target_pairs={{1,0},{2,1},{3,2},{5,4},{6,5},{7,6},{9,8},{10,9},{11,10},{13,12},{... | collective-permute-start | bytes 27656 | tf_op jit(solution)/shard_map/ppermute | solution.py:18
  102.8 6.5 %collective-permute-start.15 = (f32[3,6,1,128]{3,2,1,0:T(1,128)S(1)}, f32[3,6,1,128]{3,2,1,0:T(1,128)S(1)}, u32[]{:S(2)}, u32[]{:S(2)}) collective-permute-start(f32[3,6,1,128]{3,2,1,0:T(1,128)S(1)} %get-tuple-element.132), channel_id=1, source_target_pairs={{0,1},{1,2},{2,3},{4,5},{5,6},{6,7},{8,9},{9,10},{10,11},{12,13},{... | collective-permute-start | bytes 27656 | tf_op jit(solution)/shard_map/ppermute | solution.py:15
  110.0 5.7 %collective-permute-start.17 = (f32[6,1,16,128]{3,2,1,0:T(8,128)S(1)}, f32[6,1,16,128]{3,2,1,0:T(8,128)S(1)}, u32[]{:S(2)}, u32[]{:S(2)}) collective-permute-start(f32[6,1,16,128]{3,2,1,0:T(8,128)S(1)} %get-tuple-element.109), channel_id=1, source_target_pairs={{0,4},{4,8},{8,12},{12,16},{16,20},{20,24},{24,28},{1,5},{5,9},{9,... | collective-permute-start | bytes 147464 | tf_op jit(solution)/shard_map/ppermute | solution.py:15
  111.9 5.4 %collective-permute-start.16 = (f32[6,1,16,128]{3,2,1,0:T(8,128)S(1)}, f32[6,1,16,128]{3,2,1,0:T(8,128)S(1)}, u32[]{:S(2)}, u32[]{:S(2)}) collective-permute-start(f32[6,1,16,128]{3,2,1,0:T(8,128)S(1)} %get-tuple-element.110), channel_id=1, source_target_pairs={{4,0},{8,4},{12,8},{16,12},{20,16},{24,20},{28,24},{5,1},{9,5},{13... | collective-permute-start | bytes 147464 | tf_op jit(solution)/shard_map/ppermute | solution.py:18
  117.3 5.9 %collective-permute-start.18 = (f32[6,6,1,128]{3,2,1,0:T(1,128)S(1)}, f32[6,6,1,128]{3,2,1,0:T(1,128)S(1)}, u32[]{:S(2)}, u32[]{:S(2)}) collective-permute-start(f32[6,6,1,128]{3,2,1,0:T(1,128)S(1)} %get-tuple-element.91), channel_id=1, source_target_pairs={{1,0},{2,1},{3,2},{5,4},{6,5},{7,6},{9,8},{10,9},{11,10},{13,12},{... | collective-permute-start | bytes 55304 | tf_op jit(solution)/shard_map/ppermute | solution.py:18
  119.2 6.6 %collective-permute-start.19 = (f32[6,6,1,128]{3,2,1,0:T(1,128)S(1)}, f32[6,6,1,128]{3,2,1,0:T(1,128)S(1)}, u32[]{:S(2)}, u32[]{:S(2)}) collective-permute-start(f32[6,6,1,128]{3,2,1,0:T(1,128)S(1)} %get-tuple-element.92), channel_id=1, source_target_pairs={{0,1},{1,2},{2,3},{4,5},{5,6},{6,7},{8,9},{9,10},{10,11},{12,13},{... | collective-permute-start | bytes 55304 | tf_op jit(solution)/shard_map/ppermute | solution.py:15
  126.0 4.5 %collective-permute-start.20 = (f32[3,1,16,128]{3,2,1,0:T(8,128)S(1)}, f32[3,1,16,128]{3,2,1,0:T(8,128)S(1)}, u32[]{:S(2)}, u32[]{:S(2)}) collective-permute-start(f32[3,1,16,128]{3,2,1,0:T(8,128)S(1)} %get-tuple-element.142), channel_id=1, source_target_pairs={{4,0},{8,4},{12,8},{16,12},{20,16},{24,20},{28,24},{5,1},{9,5},{13... | collective-permute-start | bytes 73736 | tf_op jit(solution)/shard_map/ppermute | solution.py:18
  128.6 5.1 %collective-permute-start.21 = (f32[3,1,16,128]{3,2,1,0:T(8,128)S(1)}, f32[3,1,16,128]{3,2,1,0:T(8,128)S(1)}, u32[]{:S(2)}, u32[]{:S(2)}) collective-permute-start(f32[3,1,16,128]{3,2,1,0:T(8,128)S(1)} %get-tuple-element.143), channel_id=1, source_target_pairs={{0,4},{4,8},{8,12},{12,16},{16,20},{20,24},{24,28},{1,5},{5,9},{9,... | collective-permute-start | bytes 73736 | tf_op jit(solution)/shard_map/ppermute | solution.py:15
  133.7 5.9 %collective-permute-start.22 = (f32[3,6,1,128]{3,2,1,0:T(1,128)S(1)}, f32[3,6,1,128]{3,2,1,0:T(1,128)S(1)}, u32[]{:S(2)}, u32[]{:S(2)}) collective-permute-start(f32[3,6,1,128]{3,2,1,0:T(1,128)S(1)} %get-tuple-element.127), channel_id=1, source_target_pairs={{1,0},{2,1},{3,2},{5,4},{6,5},{7,6},{9,8},{10,9},{11,10},{13,12},{... | collective-permute-start | bytes 27656 | tf_op jit(solution)/shard_map/ppermute | solution.py:18
  135.7 6.5 %collective-permute-start.23 = (f32[3,6,1,128]{3,2,1,0:T(1,128)S(1)}, f32[3,6,1,128]{3,2,1,0:T(1,128)S(1)}, u32[]{:S(2)}, u32[]{:S(2)}) collective-permute-start(f32[3,6,1,128]{3,2,1,0:T(1,128)S(1)} %get-tuple-element.128), channel_id=1, source_target_pairs={{0,1},{1,2},{2,3},{4,5},{5,6},{6,7},{8,9},{9,10},{10,11},{12,13},{... | collective-permute-start | bytes 27656 | tf_op jit(solution)/shard_map/ppermute | solution.py:15
  142.9 5.7 %collective-permute-start.25 = (f32[6,1,16,128]{3,2,1,0:T(8,128)S(1)}, f32[6,1,16,128]{3,2,1,0:T(8,128)S(1)}, u32[]{:S(2)}, u32[]{:S(2)}) collective-permute-start(f32[6,1,16,128]{3,2,1,0:T(8,128)S(1)} %get-tuple-element.105), channel_id=1, source_target_pairs={{0,4},{4,8},{8,12},{12,16},{16,20},{20,24},{24,28},{1,5},{5,9},{9,... | collective-permute-start | bytes 147464 | tf_op jit(solution)/shard_map/ppermute | solution.py:15
  144.8 5.4 %collective-permute-start.24 = (f32[6,1,16,128]{3,2,1,0:T(8,128)S(1)}, f32[6,1,16,128]{3,2,1,0:T(8,128)S(1)}, u32[]{:S(2)}, u32[]{:S(2)}) collective-permute-start(f32[6,1,16,128]{3,2,1,0:T(8,128)S(1)} %get-tuple-element.106), channel_id=1, source_target_pairs={{4,0},{8,4},{12,8},{16,12},{20,16},{24,20},{28,24},{5,1},{9,5},{13... | collective-permute-start | bytes 147464 | tf_op jit(solution)/shard_map/ppermute | solution.py:18
  150.2 5.9 %collective-permute-start.26 = (f32[6,6,1,128]{3,2,1,0:T(1,128)S(1)}, f32[6,6,1,128]{3,2,1,0:T(1,128)S(1)}, u32[]{:S(2)}, u32[]{:S(2)}) collective-permute-start(f32[6,6,1,128]{3,2,1,0:T(1,128)S(1)} %get-tuple-element.87), channel_id=1, source_target_pairs={{1,0},{2,1},{3,2},{5,4},{6,5},{7,6},{9,8},{10,9},{11,10},{13,12},{... | collective-permute-start | bytes 55304 | tf_op jit(solution)/shard_map/ppermute | solution.py:18
  152.1 6.6 %collective-permute-start.27 = (f32[6,6,1,128]{3,2,1,0:T(1,128)S(1)}, f32[6,6,1,128]{3,2,1,0:T(1,128)S(1)}, u32[]{:S(2)}, u32[]{:S(2)}) collective-permute-start(f32[6,6,1,128]{3,2,1,0:T(1,128)S(1)} %get-tuple-element.88), channel_id=1, source_target_pairs={{0,1},{1,2},{2,3},{4,5},{5,6},{6,7},{8,9},{9,10},{10,11},{12,13},{... | collective-permute-start | bytes 55304 | tf_op jit(solution)/shard_map/ppermute | solution.py:15
  158.9 13.7 %copy-start.5 = (bf16[4,6,4,16,128]{4,3,2,1,0:T(8,128)(2,1)S(1)}, bf16[4,6,4,16,128]{4,3,2,1,0:T(8,128)(2,1)}, u32[]{:S(2)}) copy-start(bf16[4,6,4,16,128]{4,3,2,1,0:T(8,128)(2,1)} %param.29) | copy-start | bytes 1179652
  158.9 16.2 %copy-start.3 = (f32[3,4,16,128]{3,2,1,0:T(8,128)}, f32[3,4,16,128]{3,2,1,0:T(8,128)S(1)}, u32[]{:S(2)}) copy-start(f32[3,4,16,128]{3,2,1,0:T(8,128)S(1)} %fusion.63) | copy-start | bytes 294916
  159.0 4.6 %collective-permute-start.28 = (f32[3,1,16,128]{3,2,1,0:T(8,128)S(1)}, f32[3,1,16,128]{3,2,1,0:T(8,128)S(1)}, u32[]{:S(2)}, u32[]{:S(2)}) collective-permute-start(f32[3,1,16,128]{3,2,1,0:T(8,128)S(1)} %get-tuple-element.139), channel_id=1, source_target_pairs={{4,0},{8,4},{12,8},{16,12},{20,16},{24,20},{28,24},{5,1},{9,5},{13... | collective-permute-start | bytes 73736 | tf_op jit(solution)/shard_map/ppermute | solution.py:18
  161.6 5.1 %collective-permute-start.29 = (f32[3,1,16,128]{3,2,1,0:T(8,128)S(1)}, f32[3,1,16,128]{3,2,1,0:T(8,128)S(1)}, u32[]{:S(2)}, u32[]{:S(2)}) collective-permute-start(f32[3,1,16,128]{3,2,1,0:T(8,128)S(1)} %get-tuple-element.140), channel_id=1, source_target_pairs={{0,4},{4,8},{8,12},{12,16},{16,20},{20,24},{24,28},{1,5},{5,9},{9,... | collective-permute-start | bytes 73736 | tf_op jit(solution)/shard_map/ppermute | solution.py:15
  166.8 6.3 %collective-permute-start.30 = (f32[3,6,1,128]{3,2,1,0:T(1,128)S(1)}, f32[3,6,1,128]{3,2,1,0:T(1,128)S(1)}, u32[]{:S(2)}, u32[]{:S(2)}) collective-permute-start(f32[3,6,1,128]{3,2,1,0:T(1,128)S(1)} %get-tuple-element.123), channel_id=1, source_target_pairs={{1,0},{2,1},{3,2},{5,4},{6,5},{7,6},{9,8},{10,9},{11,10},{13,12},{... | collective-permute-start | bytes 27656 | tf_op jit(solution)/shard_map/ppermute | solution.py:18
  168.7 6.5 %collective-permute-start.31 = (f32[3,6,1,128]{3,2,1,0:T(1,128)S(1)}, f32[3,6,1,128]{3,2,1,0:T(1,128)S(1)}, u32[]{:S(2)}, u32[]{:S(2)}) collective-permute-start(f32[3,6,1,128]{3,2,1,0:T(1,128)S(1)} %get-tuple-element.124), channel_id=1, source_target_pairs={{0,1},{1,2},{2,3},{4,5},{5,6},{6,7},{8,9},{9,10},{10,11},{12,13},{... | collective-permute-start | bytes 27656 | tf_op jit(solution)/shard_map/ppermute | solution.py:15
where the time goes:
time: 179 us
  starting transfers between devices  86 us (48%)
  waiting for transfers between devices  39 us (22%)
  blocking collectives  32.8 us (18%)
  other arithmetic  13.3 us (7%)
  local copies, waits for them, and re-layouts  5.78 us (3%)
    ppermute x16, starting transfers between devices, with_halo(): lax.ppermute(lax.slice_in_dim(block, block.shape[dim] - width, None, axis...  45.8 us
    ppermute x16, starting transfers between devices, with_halo(): lax.ppermute(lax.slice_in_dim(block, 0, width, axis=dim), axis, backward)  40.2 us
    ppermute x16, waiting for transfers between devices, with_halo(): lax.ppermute(lax.slice_in_dim(block, block.shape[dim] - width, None, axis...  34.1 us
    all_gather x1, blocking collectives, per_device(): lax.all_gather(rows, 'tile', axis=1, tiled=True)  12.2 us
    all_gather x1, blocking collectives, per_device(): lax.all_gather(station_cell, 'tile', axis=0, tiled=True)  11.7 us
    all_gather x1, blocking collectives, per_device(): lax.all_gather(owners, 'tile', axis=0, tiled=True)  8.99 us
    scatter-add x1, other arithmetic, per_device(): jnp.zeros((steps * 3, surface + 1), jnp.float32).at[:, target].add(all_rows)  6.9 us
    ppermute x16, waiting for transfers between devices, with_halo(): lax.ppermute(lax.slice_in_dim(block, 0, width, axis=dim), axis, backward)  4.89 us
  transfers between devices with their start and end apart: 32, of which 15 were waited for; matrix products, arithmetic and copies ran while one was open for 5% of the time, Pallas kernels for 0%

commit v1 on v0

v1 whole, which is shorter than its diff:
```python
import functools

import jax
import jax.numpy as jnp
from jax import lax
from jax.experimental import pallas as pl
from jax.experimental.pallas import tpu as pltpu
from jax.sharding import PartitionSpec as P

courant = 0.2
mech_weights = (2.0, 3.0, 4.0)
MESH = pl.DeviceIdType.MESH

x_comps = (0, 3, 4)
z_comps = (4, 5, 2)
y_comps = (3, 1, 5)
corner_comps = (0, 3, 4, 5, 2)
step_of = (-1, 1)


def steps_kernel(
    n_tile,
    n_depth,
    relax,
    time_index,
    stress_in,
    velocity_in,
    buoyancy_in,
    owner_in,
    cell_in,
    residual_in,
    lame_in,
    qinv_in,
    memory_in,
    fwd_in,
    velocity_out,
    stress_out,
    memory_out,
    kernel_out,
    stress,
    velocity,
    buoyancy,
    owner,
    cell,
    residual,
    lame,
    qinv,
    memory,
    fwd,
    coef,
    force,
    kern,
    inject,
    gathered,
    xs,
    zs,
    cs,
    xr,
    zr,
    cr,
    in_sem,
    out_sem,
    gs_sem,
    gr_sem,
    xs_sem,
    xr_sem,
    zs_sem,
    zr_sem,
    cs_sem,
    cr_sem,
):
    steps = fwd.shape[0]
    mechs = memory.shape[0] // 6
    cx, cz, ny = velocity.shape[1:]
    listed = owner.shape[1]
    my_t = lax.axis_index("tile")
    my_d = lax.axis_index("depth")

    loads = []
    for number, (src, dst) in enumerate(
        (
            (stress_in, stress),
            (velocity_in, velocity),
            (buoyancy_in, buoyancy),
            (owner_in, owner),
            (cell_in, cell),
            (residual_in, residual),
            (lame_in, lame),
            (qinv_in, qinv),
            (memory_in, memory),
            (fwd_in, fwd),
        )
    ):
        copy = pltpu.make_async_copy(src, dst, in_sem.at[number])
        copy.start()
        loads.append(copy)

    has_t = (my_t > 0, my_t < n_tile - 1)
    has_d = (my_d > 0, my_d < n_depth - 1)
    top = my_d == 0

    barrier = pltpu.get_barrier_semaphore()

    def greet(device, amount=1):
        pl.semaphore_signal(barrier, inc=amount, device_id=device, device_id_type=MESH)

    meets = []
    for other in range(2):
        meets.append((has_d[other], my_t, my_d + step_of[other]))
        for side in range(2):
            meets.append(
                (
                    jnp.logical_and(has_t[side], has_d[other]),
                    my_t + step_of[side],
                    my_d + step_of[other],
                )
            )
    for side in range(2):
        meets.append(
            (jnp.logical_and(has_t[side], jnp.logical_not(top)), my_t + step_of[side], my_d)
        )
    for here, to_t, to_d in meets:
        pl.when(here)(lambda: greet((to_t, to_d)))

    @pl.when(top)
    def _():
        for hop in range(1, n_tile):
            greet((lax.rem(my_t + hop, n_tile), my_d))

    for side in range(2):

        @pl.when(jnp.logical_not(has_t[side]))
        def _():
            xr[:, side] = jnp.zeros((steps, 7, cz, ny), jnp.float32)

        @pl.when(jnp.logical_not(has_d[side]))
        def _():
            zr[:, side] = jnp.zeros((steps, 7, cx, 1, ny), jnp.float32)

        for other in range(2):

            @pl.when(jnp.logical_not(jnp.logical_and(has_t[side], has_d[other])))
            def _():
                cr[:, side, other] = jnp.zeros((steps, 5, 1, ny), jnp.float32)

    def gather_copy(hop):
        return pltpu.make_async_remote_copy(
            src_ref=gathered.at[0],
            dst_ref=gathered.at[hop],
            send_sem=gs_sem.at[hop],
            recv_sem=gr_sem.at[hop],
            device_id=(lax.rem(my_t + hop, n_tile), my_d),
            device_id_type=MESH,
        )

    def x_copy(step, side):
        comps = 7 if step == 0 else 6
        return pltpu.make_async_remote_copy(
            src_ref=xs.at[step, side, pl.ds(0, comps)],
            dst_ref=xr.at[step, 1 - side, pl.ds(0, comps)],
            send_sem=xs_sem.at[step, side],
            recv_sem=xr_sem.at[step, 1 - side],
            device_id=(my_t + step_of[side], my_d),
            device_id_type=MESH,
        )

    def z_copy(step, side):
        comps = 7 if step == 0 else 6
        return pltpu.make_async_remote_copy(
            src_ref=zs.at[step, side, pl.ds(0, comps)],
            dst_ref=zr.at[step, 1 - side, pl.ds(0, comps)],
            send_sem=zs_sem.at[step, side],
            recv_sem=zr_sem.at[step, 1 - side],
            device_id=(my_t, my_d + step_of[side]),
            device_id_type=MESH,
        )

    def corner_copy(step, side, other):
        return pltpu.make_async_remote_copy(
            src_ref=cs.at[step, side, other],
            dst_ref=cr.at[step, 1 - side, 1 - other],
            send_sem=cs_sem.at[step, side, other],
            recv_sem=cr_sem.at[step, 1 - side, 1 - other],
            device_id=(my_t + step_of[side], my_d + step_of[other]),
            device_id_type=MESH,
        )

    shape = (cx, cz, ny)
    at_z = lax.broadcasted_iota(jnp.int32, shape, 1)
    at_y = lax.broadcasted_iota(jnp.int32, shape, 2)
    z_first, z_last = at_z == 0, at_z == cz - 1
    y_first, y_last = at_y == 0, at_y == ny - 1
    ends_x = (0, cx - 1)
    ends_z = (0, cz - 1)

    def diff_y(field):
        after = jnp.where(y_last, 0.0, pltpu.roll(field, ny - 1, 2))
        before = jnp.where(y_first, 0.0, pltpu.roll(field, 1, 2))
        return after - before

    def diff_z(field, low, high):
        after = jnp.where(z_last, high, pltpu.roll(field, cz - 1, 1))
        before = jnp.where(z_first, low, pltpu.roll(field, 1, 1))
        return after - before

    def diff_x(field, low, high):
        return jnp.concatenate([field[1:], high], axis=0) - jnp.concatenate(
            [low, field[:-1]], axis=0
        )

    def send_corners(step):
        for side in range(2):
            for other in range(2):

                @pl.when(jnp.logical_and(has_t[side], has_d[other]))
                def _():
                    for slot, comp in enumerate(corner_comps):
                        cs[step, side, other, slot] = stress[
                            comp, ends_x[side], pl.ds(ends_z[other], 1), :
                        ]
                    corner_copy(step, side, other).start()

    def send_sides(step):
        scale = (0.5 * courant) * buoyancy[...]
        none_x = jnp.zeros((1, cz, ny), jnp.float32)
        for comp in range(3):
            sx = stress[x_comps[comp]]
            sz = stress[z_comps[comp]]
            change = (
                diff_x(sx, none_x, none_x)
                + diff_y(stress[y_comps[comp]])
                + diff_z(sz, 0.0, 0.0)
            )
            part = velocity[comp] + scale * change
            velocity[comp] = part
            for side in range(2):
                xs[step, side, comp] = part[ends_x[side]]
                xs[step, side, 3 + comp] = sx[ends_x[side]]
                end = ends_z[side]
                zs[step, side, comp] = part[:, end : end + 1, :]
                zs[step, side, 3 + comp] = sz[:, end : end + 1, :]
        if step == 0:
            for side in range(2):
                xs[step, side, 6] = scale[ends_x[side]]
                end = ends_z[side]
                zs[step, side, 6] = scale[:, end : end + 1, :]
        for side in range(2):
            pl.when(has_d[side])(lambda: z_copy(step, side).start())
            pl.when(has_t[side])(lambda: x_copy(step, side).start())

    def wait_halo(step):
        for side in range(2):
            pl.when(has_d[side])(lambda: z_copy(step, 1 - side).wait_recv())
            pl.when(has_t[side])(lambda: x_copy(step, 1 - side).wait_recv())
            for other in range(2):
                pl.when(jnp.logical_and(has_t[side], has_d[other]))(
                    lambda: corner_copy(step, 1 - side, 1 - other).wait_recv()
                )

    def wait_sent(step):
        for side in range(2):
            pl.when(has_d[side])(lambda: z_copy(step, side).wait_send())
            pl.when(has_t[side])(lambda: x_copy(step, side).wait_send())
            for other in range(2):
                pl.when(jnp.logical_and(has_t[side], has_d[other]))(
                    lambda: corner_copy(step, side, other).wait_send()
                )

    keeps = [1.0 - relax[mech] for mech in range(mechs)]
    pushes = [relax[mech] * mech_weights[mech] for mech in range(mechs)]
    push_all = pushes[0]
    for push in pushes[1:]:
        push_all = push_all + push

    peers = jnp.where(top, n_tile - 1, 0)
    for here, _, _ in meets:
        peers = peers + jnp.where(here, 1, 0)
    pl.semaphore_wait(barrier, peers)

    for number in (3, 4, 5):
        loads[number].wait()

    @pl.when(top)
    def _():
        gathered[0, 8:16] = jnp.zeros((8, listed), jnp.float32)
        for step in range(steps):
            gathered[0, 3 * step : 3 * step + 3] = residual[time_index[step]]
        gathered[0, 3 * steps : 3 * steps + 1] = (owner[...] * (cx * ny) + cell[...]).astype(
            jnp.float32
        )
        for hop in range(1, n_tile):
            gather_copy(hop).start()

    loads[0].wait()
    send_corners(0)
    loads[1].wait()
    loads[2].wait()
    send_sides(0)

    loads[6].wait()
    loads[7].wait()
    lam, shear = lame[0], lame[1]
    twist = 2.0 * shear
    shape_part = twist * qinv[0]
    bulk_part = (lam + (2.0 / 3.0) * shear) * qinv[1] - shape_part * (1.0 / 3.0)
    coef[0] = shape_part
    coef[1] = bulk_part
    kern[...] = jnp.zeros(shape, jnp.float32)

    @pl.when(top)
    def _():
        for hop in range(1, n_tile):
            gather_copy(hop).wait_recv()
        rows = jnp.concatenate([gathered[hop] for hop in range(n_tile)], axis=1)
        target = rows[3 * steps : 3 * steps + 1].astype(jnp.int32)
        total = n_tile * listed
        at_cell = lax.broadcasted_iota(jnp.int32, (ny, total), 0)
        hot = jnp.where(at_cell == lax.rem(target, ny), 1.0, 0.0).astype(jnp.bfloat16)
        local = target - (my_t * cx - 1) * ny
        high = rows.astype(jnp.bfloat16).astype(jnp.float32)
        rest = rows - high
        middle = rest.astype(jnp.bfloat16).astype(jnp.float32)
        low = rest - middle
        sides = []
        for part in (high, middle, low):
            for layer in range(cx + 2):
                inside = jnp.logical_and(local >= layer * ny, local < (layer + 1) * ny)
                sides.append(jnp.where(inside, part, 0.0).astype(jnp.bfloat16))
        found = lax.dot_general(
            jnp.concatenate(sides, axis=0),
            hot,
            (((1,), (1,)), ((), ())),
            preferred_element_type=jnp.float32,
        )
        third = (cx + 2) * 16
        found = found[:third] + found[third : 2 * third] + found[2 * third :]
        for layer in range(cx + 2):
            inject[layer] = found[16 * layer : 16 * layer + 16]

    @pl.when(jnp.logical_not(top))
    def _():
        inject[...] = jnp.zeros((cx + 2, 16, ny), jnp.float32)

    loads[8].wait()
    loads[9].wait()

    stores = []

    def store(src, dst):
        copy = pltpu.make_async_copy(src, dst, out_sem.at[len(stores)])
        copy.start()
        stores.append(copy)

    edge = lax.broadcasted_iota(jnp.int32, (1, cz, ny), 1)
    edge_ends = (edge == 0, edge == cz - 1)
    for step in range(steps):
        last = step == steps - 1
        base = []
        for comp in range(6):
            total = keeps[0] * memory[comp]
            for mech in range(1, mechs):
                total = total + keeps[mech] * memory[6 * mech + comp]
            base.append(total)
        for comp in range(6):
            force[comp] = base[comp]

        wait_halo(step)

        scale = (0.5 * courant) * buoyancy[...]
        x_scale = [xr[0, side, 6] for side in range(2)]
        z_scale = [zr[0, side, 6] for side in range(2)]
        grads_x, grads_y, grads_z = [], [], []
        for comp in range(3):
            own = velocity[comp]
            row = 3 * step + comp
            signs = (-1.0, 1.0)
            around_x, around_z = [], []
            extra = []
            for side in range(2):
                sx_end = stress[x_comps[comp], ends_x[side]]
                halo = xr[step, side, comp] - signs[side] * x_scale[side] * sx_end
                fix = jnp.zeros((cz, ny), jnp.float32)
                for other in range(2):
                    at_corner = cr[step, side, other, corner_comps.index(z_comps[comp])]
                    fix = fix + jnp.where(edge_ends[other][0], signs[other] * at_corner, 0.0)
                push_in = inject[(0, cx + 1)[side], row : row + 1, :] * (2.0 / courant)
                fix = fix + jnp.where(edge_ends[0][0], push_in, 0.0)
                around_x.append((halo + x_scale[side] * fix)[None])
                extra.append((signs[side] * xr[step, side, 3 + comp])[None])

                sz_end = stress[z_comps[comp], :, pl.ds(ends_z[side], 1), :]
                corner_row = corner_comps.index(x_comps[comp])
                at_low = cr[step, 0, side, corner_row][None]
                at_high = cr[step, 1, side, corner_row][None]
                middle = jnp.zeros((cx - 2, 1, ny), jnp.float32)
                if cx > 1:
                    fix = jnp.concatenate([-at_low, middle, at_high], axis=0)
                else:
                    fix = at_high - at_low
                around_z.append(
                    zr[step, side, comp] + z_scale[side] * (fix - signs[side] * sz_end)
                )
            if cx > 1:
                change = jnp.concatenate(
                    [extra[0], jnp.zeros((cx - 2, cz, ny), jnp.float32), extra[1]], axis=0
                )
            else:
                change = extra[0] + extra[1]
            push_in = inject[1 : cx + 1, row : row + 1, :] * (2.0 / courant)
            change = change + jnp.where(z_first, push_in - zr[step, 0, 3 + comp], 0.0)
            change = change + jnp.where(z_last, zr[step, 1, 3 + comp], 0.0)
            own = own + scale * change
            velocity[comp] = own
            grads_x.append(diff_x(own, around_x[0], around_x[1]))
            grads_y.append(diff_y(own))
            grads_z.append(diff_z(own, around_z[0], around_z[1]))
        if last:
            store(velocity, velocity_out)
        strain = [
            0.5 * grads_x[0],
            0.5 * grads_y[1],
            0.5 * grads_z[2],
            0.25 * (grads_y[0] + grads_x[1]),
            0.25 * (grads_z[0] + grads_x[2]),
            0.25 * (grads_z[1] + grads_y[2]),
        ]
        theta = strain[0] + strain[1] + strain[2]
        bulk = coef[1] * theta
        pressure = lame[0] * theta
        weighted = kern[...]
        for comp in range(6):
            push = coef[0] * strain[comp]
            grow = 2.0 * lame[1] * strain[comp]
            if comp < 3:
                push = push + bulk
                grow = grow + pressure
            total = force[comp] - push_all * push
            force[comp] = push
            stress[comp] = stress[comp] + courant * (grow + total)
            weighted = weighted + total * fwd[step, comp].astype(jnp.float32)
        if last:
            store(stress, stress_out)
            kern[...] = courant * weighted
            store(kern, kernel_out)
        else:
            kern[...] = weighted
            send_corners(step + 1)
            send_sides(step + 1)
        for mech in range(mechs):
            for comp in range(6):
                index = 6 * mech + comp
                memory[index] = keeps[mech] * memory[index] - pushes[mech] * force[comp]
            if last:
                rows = pl.ds(6 * mech, 6)
                store(memory.at[rows], memory_out.at[rows])

    for step in range(steps):
        wait_sent(step)

    @pl.when(top)
    def _():
        for hop in range(1, n_tile):
            gather_copy(hop).wait_send()

    for copy in stores:
        copy.wait()


def per_device(
    n_tile,
    n_depth,
    velocity,
    stress,
    memory,
    buoyancy,
    lame,
    qinv,
    relax,
    fwd_strain,
    residual,
    station_owner,
    station_cell,
    time_index,
):
    steps = fwd_strain.shape[0]
    mechs = relax.shape[0]
    cx, cz, ny = buoyancy.shape
    listed = station_cell.shape[0]
    f32 = jnp.float32
    owner = station_owner.reshape(1, listed)
    cell = station_cell.reshape(1, listed)
    any_spec = pl.BlockSpec(memory_space=pl.ANY)
    smem_spec = pl.BlockSpec(memory_space=pltpu.SMEM)
    operands = (
        relax,
        time_index,
        stress,
        velocity,
        buoyancy,
        owner,
        cell,
        residual,
        lame,
        qinv,
        memory,
        fwd_strain,
    )
    dma = pltpu.SemaphoreType.DMA
    return pl.pallas_call(
        functools.partial(steps_kernel, n_tile, n_depth),
        out_shape=[
            jax.ShapeDtypeStruct(velocity.shape, f32),
            jax.ShapeDtypeStruct(stress.shape, f32),
            jax.ShapeDtypeStruct(memory.shape, f32),
            jax.ShapeDtypeStruct(buoyancy.shape, f32),
        ],
        in_specs=[smem_spec] * 2 + [any_spec] * 10,
        out_specs=[any_spec] * 4,
        scratch_shapes=[pltpu.VMEM(array.shape, array.dtype) for array in operands[2:]]
        + [
            pltpu.VMEM((2, cx, cz, ny), f32),
            pltpu.VMEM((6, cx, cz, ny), f32),
            pltpu.VMEM((cx, cz, ny), f32),
            pltpu.VMEM((cx + 2, 16, ny), f32),
            pltpu.VMEM((n_tile, 16, listed), f32),
            pltpu.VMEM((steps, 2, 7, cz, ny), f32),
            pltpu.VMEM((steps, 2, 7, cx, 1, ny), f32),
            pltpu.VMEM((steps, 2, 2, 5, 1, ny), f32),
            pltpu.VMEM((steps, 2, 7, cz, ny), f32),
            pltpu.VMEM((steps, 2, 7, cx, 1, ny), f32),
            pltpu.VMEM((steps, 2, 2, 5, 1, ny), f32),
            dma((10,)),
            dma((3 + mechs,)),
            dma((n_tile,)),
            dma((n_tile,)),
            dma((steps, 2)),
            dma((steps, 2)),
            dma((steps, 2)),
            dma((steps, 2)),
            dma((steps, 2, 2)),
            dma((steps, 2, 2)),
        ],
        compiler_params=pltpu.CompilerParams(
            collective_id=0, has_side_effects=True, vmem_limit_bytes=32 * 1024 * 1024
        ),
        cost_estimate=pl.CostEstimate(
            flops=800 * cx * cz * ny * steps, bytes_accessed=2600000, transcendentals=0
        ),
    )(*operands)


def solution(mesh):
    in_specs = (
        P(None, "tile", "depth", None),
        P(None, "tile", "depth", None),
        P(None, "tile", "depth", None),
        P("tile", "depth", None),
        P(None, "tile", "depth", None),
        P(None, "tile", "depth", None),
        P(),
        P(None, None, "tile", "depth", None),
        P(None, None, "tile"),
        P("tile", None),
        P("tile"),
        P(),
    )
    out_specs = (
        P(None, "tile", "depth", None),
        P(None, "tile", "depth", None),
        P(None, "tile", "depth", None),
        P("tile", "depth", None),
    )
    return jax.shard_map(
        functools.partial(per_device, mesh.shape["tile"], mesh.shape["depth"]),
        mesh=mesh,
        in_specs=in_specs,
        out_specs=out_specs,
        check_vma=False,
    )
```

time: 179 us -> 32.4 us (0.18)
  the two profiles are of different devices: /device:TPU:12 before, /device:TPU:0 now
where the time goes in v1:
time: 32.4 us; the launch traced here: 32 us
  Pallas kernels  22.2 us (69%)
  local copies, waits for them, and re-layouts  9.08 us (28%)
  between operations  0.74 us (2%)
    pallas_call x1, Pallas kernels, per_device(): pl.pallas_call(functools.partial(steps_kernel, n_tile, n_depth), out_shap...  22.2 us
    unnamed x27, local copies, waits for them, and re-layouts  9.08 us

profile of v1, /device:TPU:0, one launch (start us, length us, event | category | flops | bytes accessed | tf_op | source)
XLA Modules:
  0.0 32.0 jit_solution(14300492583662167834)
XLA Ops:
  0.6 0.0 copy-start.3
  0.6 0.0 copy-start.7
  0.7 0.0 copy-start.8
  0.7 0.0 copy-start.9
  0.7 0.0 copy-start.10
  0.7 0.9 %copy.16.residual_in = f32[32,3,128]{2,1,0:T(4,128)S(1)} copy(f32[32,3,128]{2,0,1:T(8,128)} %param.20) | data formatting | bytes 98304 | tf_op args[8]
  1.6 0.0 copy-done.3
  1.6 0.0 copy-done.7
  1.6 0.0 copy-done.8
  1.6 0.0 copy-done.9
  1.6 0.0 copy-done.10
  1.6 0.0 copy-start
  1.6 1.1 %copy-done = f32[18,4,16,128]{3,2,1,0:T(8,128)S(1)} copy-done((f32[18,4,16,128]{3,2,1,0:T(8,128)S(1)}, f32[18,4,16,128]{3,2,1,0:T(8,128)}, u32[]{:S(2)}) %copy-start) | copy-done | bytes 589848
  2.7 0.0 copy-start.1
  2.7 1.0 %copy-done.1 = bf16[4,6,4,16,128]{4,3,2,1,0:T(8,128)(2,1)S(1)} copy-done((bf16[4,6,4,16,128]{4,3,2,1,0:T(8,128)(2,1)S(1)}, bf16[4,6,4,16,128]{4,3,2,1,0:T(8,128)(2,1)}, u32[]{:S(2)}) %copy-start.1) | copy-done | bytes 393240
  3.7 0.0 copy-start.2
  3.7 0.9 %copy-done.2 = f32[6,4,16,128]{3,2,1,0:T(8,128)S(1)} copy-done((f32[6,4,16,128]{3,2,1,0:T(8,128)S(1)}, f32[6,4,16,128]{3,2,1,0:T(8,128)}, u32[]{:S(2)}) %copy-start.2) | copy-done | bytes 196632
  4.6 0.0 copy-start.4
  4.6 0.8 %copy-done.4 = f32[2,4,16,128]{3,2,1,0:T(8,128)S(1)} copy-done((f32[2,4,16,128]{3,2,1,0:T(8,128)S(1)}, f32[2,4,16,128]{3,2,1,0:T(8,128)}, u32[]{:S(2)}) %copy-start.4) | copy-done | bytes 65560
  5.5 0.0 copy-start.5
  5.5 0.8 %copy-done.5 = f32[2,4,16,128]{3,2,1,0:T(8,128)S(1)} copy-done((f32[2,4,16,128]{3,2,1,0:T(8,128)S(1)}, f32[2,4,16,128]{3,2,1,0:T(8,128)}, u32[]{:S(2)}) %copy-start.5) | copy-done | bytes 65560
  6.3 0.0 copy-start.6
  6.3 0.8 %copy-done.6 = f32[4,16,128]{2,1,0:T(8,128)S(1)} copy-done((f32[4,16,128]{2,1,0:T(8,128)S(1)}, f32[4,16,128]{2,1,0:T(8,128)}, u32[]{:S(2)}) %copy-start.6) | copy-done | bytes 32792
  7.1 22.2 %shard_map.147 = (f32[3,4,16,128]{3,2,1,0:T(8,128)S(1)}, f32[6,4,16,128]{3,2,1,0:T(8,128)S(1)}, f32[18,4,16,128]{3,2,1,0:T(8,128)S(1)}, f32[4,16,128]{2,1,0:T(8,128)S(1)}) custom-call(f32[3]{0:T(128)S(1)} %copy-done.7, s32[4]{0:T(128)S(1)} %copy-done.8, f32[6,4,16,128]{3,2,1,0:T(8,128)S(1)} %copy-done.2, f32[3,4,16,128]{3,2,1,0:T(8,128)S(1)} %copy-done.3, ...), custom_call_target="tpu_custom_call" | custom-call | flops 26214400 | bytes 2600000 | tf_op jit(solution)/shard_map/pallas_call | solution.py:509
  29.2 0.6 %copy.21 = f32[3,4,16,128]{3,2,1,0:T(8,128)} copy(f32[3,4,16,128]{3,2,1,0:T(8,128)S(1)} %get-tuple-element.8) | data formatting | bytes 196608
  29.9 0.7 %copy.22 = f32[6,4,16,128]{3,2,1,0:T(8,128)} copy(f32[6,4,16,128]{3,2,1,0:T(8,128)S(1)} %get-tuple-element.9) | data formatting | bytes 393216
  30.6 0.8 %copy.23 = f32[18,4,16,128]{3,2,1,0:T(8,128)} copy(f32[18,4,16,128]{3,2,1,0:T(8,128)S(1)} %get-tuple-element.10) | data formatting | bytes 1179648
  31.4 0.6 %copy.24 = f32[4,16,128]{2,1,0:T(8,128)} copy(f32[4,16,128]{2,1,0:T(8,128)S(1)} %get-tuple-element.11) | data formatting | bytes 65536
Async XLA Ops:
  0.6 0.9 %copy-start.3 = (f32[3,4,16,128]{3,2,1,0:T(8,128)S(1)}, f32[3,4,16,128]{3,2,1,0:T(8,128)}, u32[]{:S(2)}) copy-start(f32[3,4,16,128]{3,2,1,0:T(8,128)} %velocity_in.1) | copy-start | bytes 294916
  0.6 0.9 %copy-start.7 = (f32[3]{0:T(128)S(1)}, f32[3]{0:T(128)}, u32[]{:S(2)}) copy-start(f32[3]{0:T(128)} %relax.1) | copy-start | bytes 40
  0.7 0.9 %copy-start.8 = (s32[4]{0:T(128)S(1)}, s32[4]{0:T(128)}, u32[]{:S(2)}) copy-start(s32[4]{0:T(128)} %time_index.1) | copy-start | bytes 52
  0.7 0.9 %copy-start.9 = (s32[128,1]{0,1:T(1,128)S(1)}, s32[128,1]{0,1:T(1,128)}, u32[]{:S(2)}) copy-start(s32[128,1]{0,1:T(1,128)} %param.21) | copy-start | bytes 1540
  0.7 0.9 %copy-start.10 = (s32[128]{0:T(128)S(1)}, s32[128]{0:T(128)}, u32[]{:S(2)}) copy-start(s32[128]{0:T(128)} %param.22) | copy-start | bytes 1540
  1.6 1.1 %copy-start = (f32[18,4,16,128]{3,2,1,0:T(8,128)S(1)}, f32[18,4,16,128]{3,2,1,0:T(8,128)}, u32[]{:S(2)}) copy-start(f32[18,4,16,128]{3,2,1,0:T(8,128)} %memory_in.1) | copy-start | bytes 1769476
  2.7 1.0 %copy-start.1 = (bf16[4,6,4,16,128]{4,3,2,1,0:T(8,128)(2,1)S(1)}, bf16[4,6,4,16,128]{4,3,2,1,0:T(8,128)(2,1)}, u32[]{:S(2)}) copy-start(bf16[4,6,4,16,128]{4,3,2,1,0:T(8,128)(2,1)} %fwd_in.1) | copy-start | bytes 1179652
  3.7 0.9 %copy-start.2 = (f32[6,4,16,128]{3,2,1,0:T(8,128)S(1)}, f32[6,4,16,128]{3,2,1,0:T(8,128)}, u32[]{:S(2)}) copy-start(f32[6,4,16,128]{3,2,1,0:T(8,128)} %stress_in.1) | copy-start | bytes 589828
  4.6 0.8 %copy-start.4 = (f32[2,4,16,128]{3,2,1,0:T(8,128)S(1)}, f32[2,4,16,128]{3,2,1,0:T(8,128)}, u32[]{:S(2)}) copy-start(f32[2,4,16,128]{3,2,1,0:T(8,128)} %lame_in.1) | copy-start | bytes 196612
  5.5 0.8 %copy-start.5 = (f32[2,4,16,128]{3,2,1,0:T(8,128)S(1)}, f32[2,4,16,128]{3,2,1,0:T(8,128)}, u32[]{:S(2)}) copy-start(f32[2,4,16,128]{3,2,1,0:T(8,128)} %qinv_in.1) | copy-start | bytes 196612
  6.3 0.8 %copy-start.6 = (f32[4,16,128]{2,1,0:T(8,128)S(1)}, f32[4,16,128]{2,1,0:T(8,128)}, u32[]{:S(2)}) copy-start(f32[4,16,128]{2,1,0:T(8,128)} %buoyancy_in.1) | copy-start | bytes 98308

commit v2 on v1

--- a/solution.py
+++ b/solution.py
@@ -21,8 +21,8 @@
 def steps_kernel(
     n_tile,
     n_depth,
-    relax,
-    time_index,
+    relax_in,
+    time_index_in,
     stress_in,
     velocity_in,
     buoyancy_in,
@@ -33,23 +33,22 @@
     qinv_in,
     memory_in,
     fwd_in,
-    velocity_out,
-    stress_out,
-    memory_out,
-    kernel_out,
+    velocity,
     stress,
-    velocity,
+    memory,
+    kern,
     buoyancy,
     owner,
     cell,
     residual,
     lame,
     qinv,
-    memory,
     fwd,
+    relax,
+    time_index,
     coef,
     force,
-    kern,
+    sums,
     inject,
     gathered,
     xs,
@@ -59,7 +58,6 @@
     zr,
     cr,
     in_sem,
-    out_sem,
     gs_sem,
     gr_sem,
     xs_sem,
@@ -73,27 +71,9 @@
     mechs = memory.shape[0] // 6
     cx, cz, ny = velocity.shape[1:]
     listed = owner.shape[1]
+    blocks = gathered.shape[0]
     my_t = lax.axis_index("tile")
     my_d = lax.axis_index("depth")
-
-    loads = []
-    for number, (src, dst) in enumerate(
-        (
-            (stress_in, stress),
-            (velocity_in, velocity),
-            (buoyancy_in, buoyancy),
-            (owner_in, owner),
-            (cell_in, cell),
-            (residual_in, residual),
-            (lame_in, lame),
-            (qinv_in, qinv),
-            (memory_in, memory),
-            (fwd_in, fwd),
-        )
-    ):
-        copy = pltpu.make_async_copy(src, dst, in_sem.at[number])
-        copy.start()
-        loads.append(copy)
 
     has_t = (my_t > 0, my_t < n_tile - 1)
     has_d = (my_d > 0, my_d < n_depth - 1)
@@ -127,6 +107,27 @@
         for hop in range(1, n_tile):
             greet((lax.rem(my_t + hop, n_tile), my_d))
 
+    loads = []
+    for number, (src, dst) in enumerate(
+        (
+            (stress_in, stress),
+            (velocity_in, velocity),
+            (buoyancy_in, buoyancy),
+            (owner_in, owner),
+            (cell_in, cell),
+            (residual_in, residual),
+            (lame_in, lame),
+            (qinv_in, qinv),
+            (memory_in, memory),
+            (fwd_in, fwd),
+            (time_index_in, time_index),
+            (relax_in, relax),
+        )
+    ):
+        copy = pltpu.make_async_copy(src, dst, in_sem.at[number])
+        copy.start()
+        loads.append(copy)
+
     for side in range(2):
 
         @pl.when(jnp.logical_not(has_t[side]))
@@ -143,23 +144,23 @@
             def _():
                 cr[:, side, other] = jnp.zeros((steps, 5, 1, ny), jnp.float32)
 
-    def gather_copy(hop):
+    def gather_copy(block, hop):
         return pltpu.make_async_remote_copy(
-            src_ref=gathered.at[0],
-            dst_ref=gathered.at[hop],
-            send_sem=gs_sem.at[hop],
-            recv_sem=gr_sem.at[hop],
+            src_ref=gathered.at[block, 0],
+            dst_ref=gathered.at[block, hop],
+            send_sem=gs_sem.at[block, hop],
+            recv_sem=gr_sem.at[block, hop],
             device_id=(lax.rem(my_t + hop, n_tile), my_d),
             device_id_type=MESH,
         )
 
-    def x_copy(step, side):
-        comps = 7 if step == 0 else 6
+    def x_copy(step, side, early):
+        first, comps = (0, 3) if early else (3, 4 if step == 0 else 3)
         return pltpu.make_async_remote_copy(
-            src_ref=xs.at[step, side, pl.ds(0, comps)],
-            dst_ref=xr.at[step, 1 - side, pl.ds(0, comps)],
-            send_sem=xs_sem.at[step, side],
-            recv_sem=xr_sem.at[step, 1 - side],
+            src_ref=xs.at[step, side, pl.ds(first, comps)],
+            dst_ref=xr.at[step, 1 - side, pl.ds(first, comps)],
+            send_sem=xs_sem.at[step, side, int(early)],
+            recv_sem=xr_sem.at[step, 1 - side, int(early)],
             device_id=(my_t + step_of[side], my_d),
             device_id_type=MESH,
         )
@@ -219,6 +220,14 @@
                             comp, ends_x[side], pl.ds(ends_z[other], 1), :
                         ]
                     corner_copy(step, side, other).start()
+
+        for side in range(2):
+
+            @pl.when(has_t[side])
+            def _():
+                for slot, comp in enumerate(x_comps):
+                    xs[step, side, slot] = stress[comp, ends_x[side]]
+                x_copy(step, side, True).start()
 
     def send_sides(step):
         scale = (0.5 * courant) * buoyancy[...]
@@ -234,8 +243,7 @@
             part = velocity[comp] + scale * change
             velocity[comp] = part
             for side in range(2):
-                xs[step, side, comp] = part[ends_x[side]]
-                xs[step, side, 3 + comp] = sx[ends_x[side]]
+                xs[step, side, 3 + comp] = part[ends_x[side]]
                 end = ends_z[side]
                 zs[step, side, comp] = part[:, end : end + 1, :]
                 zs[step, side, 3 + comp] = sz[:, end : end + 1, :]
@@ -246,12 +254,14 @@
                 zs[step, side, 6] = scale[:, end : end + 1, :]
         for side in range(2):
             pl.when(has_d[side])(lambda: z_copy(step, side).start())
-            pl.when(has_t[side])(lambda: x_copy(step, side).start())
+            pl.when(has_t[side])(lambda: x_copy(step, side, False).start())
 
     def wait_halo(step):
         for side in range(2):
             pl.when(has_d[side])(lambda: z_copy(step, 1 - side).wait_recv())
-            pl.when(has_t[side])(lambda: x_copy(step, 1 - side).wait_recv())
+            pl.when(has_t[side])(
+                lambda: [x_copy(step, 1 - side, early).wait_recv() for early in (True, False)] and None
+            )
             for other in range(2):
                 pl.when(jnp.logical_and(has_t[side], has_d[other]))(
                     lambda: corner_copy(step, 1 - side, 1 - other).wait_recv()
@@ -260,42 +270,48 @@
     def wait_sent(step):
         for side in range(2):
             pl.when(has_d[side])(lambda: z_copy(step, side).wait_send())
-            pl.when(has_t[side])(lambda: x_copy(step, side).wait_send())
+            pl.when(has_t[side])(
+                lambda: [x_copy(step, side, early).wait_send() for early in (True, False)] and None
+            )
             for other in range(2):
                 pl.when(jnp.logical_and(has_t[side], has_d[other]))(
                     lambda: corner_copy(step, side, other).wait_send()
                 )
 
-    keeps = [1.0 - relax[mech] for mech in range(mechs)]
-    pushes = [relax[mech] * mech_weights[mech] for mech in range(mechs)]
-    push_all = pushes[0]
-    for push in pushes[1:]:
-        push_all = push_all + push
-
     peers = jnp.where(top, n_tile - 1, 0)
     for here, _, _ in meets:
         peers = peers + jnp.where(here, 1, 0)
     pl.semaphore_wait(barrier, peers)
 
-    for number in (3, 4, 5):
+    for number in (3, 4, 5, 10):
         loads[number].wait()
+
+    def send_stations(block):
+        for hop in range(1, n_tile):
+            gather_copy(block, hop).start()
 
     @pl.when(top)
     def _():
-        gathered[0, 8:16] = jnp.zeros((8, listed), jnp.float32)
+        gathered[:, 0] = jnp.zeros((blocks, 8, listed), jnp.float32)
         for step in range(steps):
-            gathered[0, 3 * step : 3 * step + 3] = residual[time_index[step]]
-        gathered[0, 3 * steps : 3 * steps + 1] = (owner[...] * (cx * ny) + cell[...]).astype(
-            jnp.float32
-        )
-        for hop in range(1, n_tile):
-            gather_copy(hop).start()
+            for comp in range(3):
+                row = 3 * (step % 2) + comp
+                gathered[step // 2, 0, row : row + 1] = residual[
+                    comp, pl.ds(time_index[step], 1), :
+                ]
+        gathered[0, 0, 6:7] = (owner[...] * (cx * ny) + cell[...]).astype(jnp.float32)
+        send_stations(0)
 
     loads[0].wait()
     send_corners(0)
     loads[1].wait()
     loads[2].wait()
     send_sides(0)
+
+    @pl.when(top)
+    def _():
+        for block in range(1, blocks):
+            send_stations(block)
 
     loads[6].wait()
     loads[7].wait()
@@ -307,12 +323,12 @@
     coef[1] = bulk_part
     kern[...] = jnp.zeros(shape, jnp.float32)
 
-    @pl.when(top)
-    def _():
+    def place_stations(block):
         for hop in range(1, n_tile):
-            gather_copy(hop).wait_recv()
-        rows = jnp.concatenate([gathered[hop] for hop in range(n_tile)], axis=1)
-        target = rows[3 * steps : 3 * steps + 1].astype(jnp.int32)
+            gather_copy(block, hop).wait_recv()
+        rows = jnp.concatenate([gathered[block, hop] for hop in range(n_tile)], axis=1)
+        target = jnp.concatenate([gathered[0, hop, 6:7] for hop in range(n_tile)], axis=1)
+        target = target.astype(jnp.int32)
         total = n_tile * listed
         at_cell = lax.broadcasted_iota(jnp.int32, (ny, total), 0)
         hot = jnp.where(at_cell == lax.rem(target, ny), 1.0, 0.0).astype(jnp.bfloat16)
@@ -325,45 +341,45 @@
         for part in (high, middle, low):
             for layer in range(cx + 2):
                 inside = jnp.logical_and(local >= layer * ny, local < (layer + 1) * ny)
-                sides.append(jnp.where(inside, part, 0.0).astype(jnp.bfloat16))
+                sides.append(jnp.where(inside, part, 0.0))
         found = lax.dot_general(
-            jnp.concatenate(sides, axis=0),
+            jnp.concatenate(sides, axis=0).astype(jnp.bfloat16),
             hot,
             (((1,), (1,)), ((), ())),
             preferred_element_type=jnp.float32,
         )
-        third = (cx + 2) * 16
+        third = (cx + 2) * 8
         found = found[:third] + found[third : 2 * third] + found[2 * third :]
         for layer in range(cx + 2):
-            inject[layer] = found[16 * layer : 16 * layer + 16]
+            inject[layer, 8 * block : 8 * block + 8] = found[8 * layer : 8 * layer + 8]
 
     @pl.when(jnp.logical_not(top))
     def _():
-        inject[...] = jnp.zeros((cx + 2, 16, ny), jnp.float32)
+        inject[...] = jnp.zeros((cx + 2, 8 * blocks, ny), jnp.float32)
 
     loads[8].wait()
     loads[9].wait()
-
-    stores = []
-
-    def store(src, dst):
-        copy = pltpu.make_async_copy(src, dst, out_sem.at[len(stores)])
-        copy.start()
-        stores.append(copy)
+    loads[11].wait()
+    keeps = [1.0 - relax[mech] for mech in range(mechs)]
+    pushes = [relax[mech] * mech_weights[mech] for mech in range(mechs)]
+    push_all = pushes[0]
+    for push in pushes[1:]:
+        push_all = push_all + push
+
+
+    for comp in range(6):
+        total = keeps[0] * memory[comp]
+        for mech in range(1, mechs):
+            total = total + keeps[mech] * memory[6 * mech + comp]
+        sums[comp] = total
 
     edge = lax.broadcasted_iota(jnp.int32, (1, cz, ny), 1)
     edge_ends = (edge == 0, edge == cz - 1)
     for step in range(steps):
         last = step == steps - 1
-        base = []
-        for comp in range(6):
-            total = keeps[0] * memory[comp]
-            for mech in range(1, mechs):
-                total = total + keeps[mech] * memory[6 * mech + comp]
-            base.append(total)
-        for comp in range(6):
-            force[comp] = base[comp]
-
+        for block in range(blocks):
+            if step == max(0, 2 * block - 1):
+                pl.when(top)(lambda: place_stations(block))
         wait_halo(step)
 
         scale = (0.5 * courant) * buoyancy[...]
@@ -372,13 +388,13 @@
         grads_x, grads_y, grads_z = [], [], []
         for comp in range(3):
             own = velocity[comp]
-            row = 3 * step + comp
+            row = 8 * (step // 2) + 3 * (step % 2) + comp
             signs = (-1.0, 1.0)
             around_x, around_z = [], []
             extra = []
             for side in range(2):
                 sx_end = stress[x_comps[comp], ends_x[side]]
-                halo = xr[step, side, comp] - signs[side] * x_scale[side] * sx_end
+                halo = xr[step, side, 3 + comp] - signs[side] * x_scale[side] * sx_end
                 fix = jnp.zeros((cz, ny), jnp.float32)
                 for other in range(2):
                     at_corner = cr[step, side, other, corner_comps.index(z_comps[comp])]
@@ -386,7 +402,7 @@
                 push_in = inject[(0, cx + 1)[side], row : row + 1, :] * (2.0 / courant)
                 fix = fix + jnp.where(edge_ends[0][0], push_in, 0.0)
                 around_x.append((halo + x_scale[side] * fix)[None])
-                extra.append((signs[side] * xr[step, side, 3 + comp])[None])
+                extra.append((signs[side] * xr[step, side, comp])[None])
 
                 sz_end = stress[z_comps[comp], :, pl.ds(ends_z[side], 1), :]
                 corner_row = corner_comps.index(x_comps[comp])
@@ -414,8 +430,6 @@
             grads_x.append(diff_x(own, around_x[0], around_x[1]))
             grads_y.append(diff_y(own))
             grads_z.append(diff_z(own, around_z[0], around_z[1]))
-        if last:
-            store(velocity, velocity_out)
         strain = [
             0.5 * grads_x[0],
             0.5 * grads_y[1],
@@ -427,42 +441,61 @@
         theta = strain[0] + strain[1] + strain[2]
         bulk = coef[1] * theta
         pressure = lame[0] * theta
-        weighted = kern[...]
         for comp in range(6):
             push = coef[0] * strain[comp]
             grow = 2.0 * lame[1] * strain[comp]
             if comp < 3:
                 push = push + bulk
                 grow = grow + pressure
-            total = force[comp] - push_all * push
+            total = sums[comp] - push_all * push
+            sums[comp] = total
             force[comp] = push
             stress[comp] = stress[comp] + courant * (grow + total)
-            weighted = weighted + total * fwd[step, comp].astype(jnp.float32)
-        if last:
-            store(stress, stress_out)
-            kern[...] = courant * weighted
-            store(kern, kernel_out)
-        else:
-            kern[...] = weighted
+        if not last:
             send_corners(step + 1)
             send_sides(step + 1)
-        for mech in range(mechs):
-            for comp in range(6):
+        weighted = kern[...]
+        for comp in range(6):
+            weighted = weighted + sums[comp] * fwd[step, comp].astype(jnp.float32)
+        kern[...] = courant * weighted if last else weighted
+        for comp in range(6):
+            push = force[comp]
+            total = None
+            for mech in range(mechs):
                 index = 6 * mech + comp
-                memory[index] = keeps[mech] * memory[index] - pushes[mech] * force[comp]
-            if last:
-                rows = pl.ds(6 * mech, 6)
-                store(memory.at[rows], memory_out.at[rows])
+                new = keeps[mech] * memory[index] - pushes[mech] * push
+                memory[index] = new
+                if not last:
+                    ahead = keeps[mech] * new
+                    total = ahead if total is None else total + ahead
+            if not last:
+                sums[comp] = total
 
     for step in range(steps):
         wait_sent(step)
 
     @pl.when(top)
     def _():
-        for hop in range(1, n_tile):
-            gather_copy(hop).wait_send()
-
-    for copy in stores:
+        for block in range(blocks):
+            for hop in range(1, n_tile):
+                gather_copy(block, hop).wait_send()
+
+
+def hand_out(velocity, stress, memory, kern, velocity_to, stress_to, memory_to, kern_to, sem):
+    copies = [
+        pltpu.make_async_copy(src, dst, sem.at[number])
+        for number, (src, dst) in enumerate(
+            (
+                (memory, memory_to),
+                (stress, stress_to),
+                (velocity, velocity_to),
+                (kern, kern_to),
+            )
+        )
+    ]
+    for copy in copies:
+        copy.start()
+    for copy in copies:
         copy.wait()
 
 
@@ -487,11 +520,11 @@
     cx, cz, ny = buoyancy.shape
     listed = station_cell.shape[0]
     f32 = jnp.float32
+    blocks = -(-steps // 2)
     owner = station_owner.reshape(1, listed)
     cell = station_cell.reshape(1, listed)
     any_spec = pl.BlockSpec(memory_space=pl.ANY)
-    smem_spec = pl.BlockSpec(memory_space=pltpu.SMEM)
-    operands = (
+    arrays = (
         relax,
         time_index,
         stress,
@@ -499,42 +532,41 @@
         buoyancy,
         owner,
         cell,
-        residual,
+        jnp.transpose(residual, (1, 0, 2)),
         lame,
         qinv,
         memory,
         fwd_strain,
     )
+    arrays = [pltpu.with_memory_space_constraint(array, pltpu.HBM) for array in arrays]
+    held = arrays[4:10] + arrays[11:]
     dma = pltpu.SemaphoreType.DMA
-    return pl.pallas_call(
+    results = (velocity, stress, memory, buoyancy)
+    state = pl.pallas_call(
         functools.partial(steps_kernel, n_tile, n_depth),
-        out_shape=[
-            jax.ShapeDtypeStruct(velocity.shape, f32),
-            jax.ShapeDtypeStruct(stress.shape, f32),
-            jax.ShapeDtypeStruct(memory.shape, f32),
-            jax.ShapeDtypeStruct(buoyancy.shape, f32),
-        ],
-        in_specs=[smem_spec] * 2 + [any_spec] * 10,
-        out_specs=[any_spec] * 4,
-        scratch_shapes=[pltpu.VMEM(array.shape, array.dtype) for array in operands[2:]]
+        out_shape=[pltpu.VMEM(array.shape, f32) for array in results],
+        in_specs=[any_spec] * 12,
+        out_specs=[pl.BlockSpec(memory_space=pltpu.VMEM)] * 4,
+        scratch_shapes=[pltpu.VMEM(array.shape, array.dtype) for array in held]
         + [
+            pltpu.SMEM(relax.shape, f32),
+            pltpu.SMEM(time_index.shape, jnp.int32),
             pltpu.VMEM((2, cx, cz, ny), f32),
             pltpu.VMEM((6, cx, cz, ny), f32),
-            pltpu.VMEM((cx, cz, ny), f32),
-            pltpu.VMEM((cx + 2, 16, ny), f32),
-            pltpu.VMEM((n_tile, 16, listed), f32),
+            pltpu.VMEM((6, cx, cz, ny), f32),
+            pltpu.VMEM((cx + 2, 8 * blocks, ny), f32),
+            pltpu.VMEM((blocks, n_tile, 8, listed), f32),
             pltpu.VMEM((steps, 2, 7, cz, ny), f32),
             pltpu.VMEM((steps, 2, 7, cx, 1, ny), f32),
             pltpu.VMEM((steps, 2, 2, 5, 1, ny), f32),
             pltpu.VMEM((steps, 2, 7, cz, ny), f32),
             pltpu.VMEM((steps, 2, 7, cx, 1, ny), f32),
             pltpu.VMEM((steps, 2, 2, 5, 1, ny), f32),
-            dma((10,)),
-            dma((3 + mechs,)),
-            dma((n_tile,)),
-            dma((n_tile,)),
-            dma((steps, 2)),
-            dma((steps, 2)),
+            dma((12,)),
+            dma((blocks, n_tile)),
+            dma((blocks, n_tile)),
+            dma((steps, 2, 2)),
+            dma((steps, 2, 2)),
             dma((steps, 2)),
             dma((steps, 2)),
             dma((steps, 2, 2)),
@@ -546,7 +578,14 @@
         cost_estimate=pl.CostEstimate(
             flops=800 * cx * cz * ny * steps, bytes_accessed=2600000, transcendentals=0
         ),
-    )(*operands)
+    )(*arrays)
+    return pl.pallas_call(
+        hand_out,
+        out_shape=[pltpu.HBM(array.shape, f32) for array in results],
+        in_specs=[pl.BlockSpec(memory_space=pltpu.VMEM)] * 4,
+        out_specs=[any_spec] * 4,
+        scratch_shapes=[dma((4,))],
+    )(*[pltpu.with_memory_space_constraint(array, pltpu.VMEM) for array in state])
 
 
 def solution(mesh):

time: 32.4 us -> 21.5 us (0.66)
  local copies, waits for them, and re-layouts: 9.08 us -> 0 us
  Pallas kernels: 22.2 us -> 20.7 us
    unnamed x27 -> x0, local copies, waits for them, and re-layouts: 9.08 us -> none
    pallas_call x1, Pallas kernels: 22.2 us -> 19.7 us  [per_device(): pl.pallas_call(functools.partial(steps_kernel, n_tile, n_depth), out_shap...]
    pallas_call x0 -> x1, Pallas kernels: none -> 0.94 us  [per_device(): pl.pallas_call(hand_out, out_shape=[pltpu.HBM(array.shape, f32) for array...]
where the time goes in v2:
time: 21.5 us; the launch traced here: 21.3 us
  Pallas kernels  20.7 us (96%)
  between operations  0.64 us (3%)
    pallas_call x1, Pallas kernels, per_device(): pl.pallas_call(functools.partial(steps_kernel, n_tile, n_depth), out_shap...  19.7 us
    pallas_call x1, Pallas kernels, per_device(): pl.pallas_call(hand_out, out_shape=[pltpu.HBM(array.shape, f32) for array...  0.94 us

profile of v2, /device:TPU:0, one launch (start us, length us, event | category | flops | bytes accessed | tf_op | source)
XLA Modules:
  0.0 21.3 jit_solution(1888678399688454591)
XLA Ops:
  0.6 19.7 %shard_map.147 = (f32[3,4,16,128]{3,2,1,0:T(8,128)S(1)}, f32[6,4,16,128]{3,2,1,0:T(8,128)S(1)}, f32[18,4,16,128]{3,2,1,0:T(8,128)S(1)}, f32[4,16,128]{2,1,0:T(8,128)S(1)}) custom-call(f32[3]{0:T(128)} %relax_in.1, s32[4]{0:T(128)} %time_index_in.1, f32[6,4,16,128]{3,2,1,0:T(8,128)} %stress_in.1, f32[3,4,16,128]{3,2,1,0:T(8,128)} %velocity_in.1, ...), custom_call_target="tpu_custom_call" | custom-call | flops 26214400 | bytes 2600000 | tf_op jit(solution)/shard_map/pallas_call | solution.py:545
  20.4 0.9 %shard_map.148 = (f32[3,4,16,128]{3,2,1,0:T(8,128)}, f32[6,4,16,128]{3,2,1,0:T(8,128)}, f32[18,4,16,128]{3,2,1,0:T(8,128)}, f32[4,16,128]{2,1,0:T(8,128)}) custom-call(f32[3,4,16,128]{3,2,1,0:T(8,128)S(1)} %get-tuple-element.8.velocity, f32[6,4,16,128]{3,2,1,0:T(8,128)S(1)} %get-tuple-element.9.stress, f32[18,4,16,128]{3,2,1,0:T(8,128)S(1)} %get-tuple-element.10.memory, ...), custom_call_target="tpu_custom_call" | custom-call | tf_op jit(solution)/shard_map/pallas_call | solution.py:582

commit v3 on v2

--- a/solution.py
+++ b/solution.py
@@ -75,38 +75,6 @@
     my_t = lax.axis_index("tile")
     my_d = lax.axis_index("depth")
 
-    has_t = (my_t > 0, my_t < n_tile - 1)
-    has_d = (my_d > 0, my_d < n_depth - 1)
-    top = my_d == 0
-
-    barrier = pltpu.get_barrier_semaphore()
-
-    def greet(device, amount=1):
-        pl.semaphore_signal(barrier, inc=amount, device_id=device, device_id_type=MESH)
-
-    meets = []
-    for other in range(2):
-        meets.append((has_d[other], my_t, my_d + step_of[other]))
-        for side in range(2):
-            meets.append(
-                (
-                    jnp.logical_and(has_t[side], has_d[other]),
-                    my_t + step_of[side],
-                    my_d + step_of[other],
-                )
-            )
-    for side in range(2):
-        meets.append(
-            (jnp.logical_and(has_t[side], jnp.logical_not(top)), my_t + step_of[side], my_d)
-        )
-    for here, to_t, to_d in meets:
-        pl.when(here)(lambda: greet((to_t, to_d)))
-
-    @pl.when(top)
-    def _():
-        for hop in range(1, n_tile):
-            greet((lax.rem(my_t + hop, n_tile), my_d))
-
     loads = []
     for number, (src, dst) in enumerate(
         (
@@ -125,8 +93,44 @@
         )
     ):
         copy = pltpu.make_async_copy(src, dst, in_sem.at[number])
-        copy.start()
+        if number < 3:
+            copy.start()
         loads.append(copy)
+
+    has_t = (my_t > 0, my_t < n_tile - 1)
+    has_d = (my_d > 0, my_d < n_depth - 1)
+    top = my_d == 0
+
+    barrier = pltpu.get_barrier_semaphore()
+
+    def greet(device, amount=1):
+        pl.semaphore_signal(barrier, inc=amount, device_id=device, device_id_type=MESH)
+
+    meets = []
+    for other in range(2):
+        meets.append((has_d[other], my_t, my_d + step_of[other]))
+        for side in range(2):
+            meets.append(
+                (
+                    jnp.logical_and(has_t[side], has_d[other]),
+                    my_t + step_of[side],
+                    my_d + step_of[other],
+                )
+            )
+    for side in range(2):
+        meets.append(
+            (jnp.logical_and(has_t[side], jnp.logical_not(top)), my_t + step_of[side], my_d)
+        )
+    for here, to_t, to_d in meets:
+        pl.when(here)(lambda: greet((to_t, to_d)))
+
+    @pl.when(top)
+    def _():
+        for hop in range(1, n_tile):
+            greet((lax.rem(my_t + hop, n_tile), my_d))
+
+    for number in (3, 4, 5, 10, 11, 6, 7, 8, 9):
+        loads[number].start()
 
     for side in range(2):
 
@@ -482,16 +486,18 @@
 
 
 def hand_out(velocity, stress, memory, kern, velocity_to, stress_to, memory_to, kern_to, sem):
+    pairs = []
+    for first in range(0, memory.shape[0], 3):
+        rows = pl.ds(first, 3)
+        pairs.append((memory.at[rows], memory_to.at[rows]))
+    for first in (0, 3):
+        rows = pl.ds(first, 3)
+        pairs.append((stress.at[rows], stress_to.at[rows]))
+    pairs.append((velocity, velocity_to))
+    pairs.append((kern, kern_to))
     copies = [
         pltpu.make_async_copy(src, dst, sem.at[number])
-        for number, (src, dst) in enumerate(
-            (
-                (memory, memory_to),
-                (stress, stress_to),
-                (velocity, velocity_to),
-                (kern, kern_to),
-            )
-        )
+        for number, (src, dst) in enumerate(pairs)
     ]
     for copy in copies:
         copy.start()
@@ -584,7 +590,7 @@
         out_shape=[pltpu.HBM(array.shape, f32) for array in results],
         in_specs=[pl.BlockSpec(memory_space=pltpu.VMEM)] * 4,
         out_specs=[any_spec] * 4,
-        scratch_shapes=[dma((4,))],
+        scratch_shapes=[dma((2 * mechs + 4,))],
     )(*[pltpu.with_memory_space_constraint(array, pltpu.VMEM) for array in state])
 
 

time: 21.5 us -> 21.5 us (level)
  no operation moved by 1% of the time
where the time goes in v3:
time: 21.5 us; the launch traced here: 21.4 us
  Pallas kernels  20.7 us (96%)
  between operations  0.64 us (3%)
    pallas_call x1, Pallas kernels, per_device(): pl.pallas_call(functools.partial(steps_kernel, n_tile, n_depth), out_shap...  19.7 us
    pallas_call x1, Pallas kernels, per_device(): pl.pallas_call(hand_out, out_shape=[pltpu.HBM(array.shape, f32) for array...  1 us

profile of v3, /device:TPU:0, one launch (start us, length us, event | category | flops | bytes accessed | tf_op | source)
XLA Modules:
  0.0 21.4 jit_solution(7991886409045619063)
XLA Ops:
  0.6 19.7 %shard_map.147 = (f32[3,4,16,128]{3,2,1,0:T(8,128)S(1)}, f32[6,4,16,128]{3,2,1,0:T(8,128)S(1)}, f32[18,4,16,128]{3,2,1,0:T(8,128)S(1)}, f32[4,16,128]{2,1,0:T(8,128)S(1)}) custom-call(f32[3]{0:T(128)} %relax_in.1, s32[4]{0:T(128)} %time_index_in.1, f32[6,4,16,128]{3,2,1,0:T(8,128)} %stress_in.1, f32[3,4,16,128]{3,2,1,0:T(8,128)} %velocity_in.1, ...), custom_call_target="tpu_custom_call" | custom-call | flops 26214400 | bytes 2600000 | tf_op jit(solution)/shard_map/pallas_call | solution.py:551
  20.4 1.0 %shard_map.148 = (f32[3,4,16,128]{3,2,1,0:T(8,128)}, f32[6,4,16,128]{3,2,1,0:T(8,128)}, f32[18,4,16,128]{3,2,1,0:T(8,128)}, f32[4,16,128]{2,1,0:T(8,128)}) custom-call(f32[3,4,16,128]{3,2,1,0:T(8,128)S(1)} %get-tuple-element.8.velocity, f32[6,4,16,128]{3,2,1,0:T(8,128)S(1)} %get-tuple-element.9.stress, f32[18,4,16,128]{3,2,1,0:T(8,128)S(1)} %get-tuple-element.10.memory, ...), custom_call_target="tpu_custom_call" | custom-call | tf_op jit(solution)/shard_map/pallas_call | solution.py:588
